TPU v7x, 32 devices: a whole 2x2x4 slice. The times are simulated.
32 devices in a mesh: ctx: 16 (over z, x, core), head: 2 (over y).
Axes of the slice: x: 2, y: 2, z: 4, core: 2. Of those that a mesh axis runs over, the one named last changes fastest.
Arguments:
- query_rows: bfloat16 [16384, 1024], P('ctx', 'head'), may hold values from -8 to 8
- key_rows: bfloat16 [16384, 1024], P('ctx', 'head'), may hold values from -8 to 8
- value_rows: bfloat16 [16384, 1024], P('ctx', 'head'), may hold values from -6 to 6
- out_grad: bfloat16 [16384, 1024], P('ctx', 'head'), may hold values from -6 to 6
- out_weight: bfloat16 [1024, 1024], P('head'), may hold values from -0.1875 to 0.1875
- neighbours: int32 [128, 12], replicated, may hold values from 0 to 127, as said below
- counts: int32 [128], replicated, may hold values from 3 to 12, as said below
Outputs:
- query_grad: bfloat16 [16384, 1024], P('ctx', 'head')
- key_grad: bfloat16 [16384, 1024], P('ctx', 'head')
- value_grad: bfloat16 [16384, 1024], P('ctx', 'head')
- weight_grad: float32 [1024, 1024], P('head')
Inputs may be any that keep to these rules, and one draw needn't show every extreme that they name: `neighbours`: row g names block g in slot 0, then distinct blocks held by ctx indices g // 8 - 1 to g // 8 + 1; slots 1 and 2 include a block of each of the ctx indices g // 8 - 1 and g // 8 + 1 that exists; slots from counts[g] on hold g again. `counts`: block 0 uses all 12 slots.
All inputs are finite; a program needn't handle non-finite values.
Results may differ from a plain program's by a relative error of at most 0.012.
The roundings to bfloat16 on the way count: a program that leaves them out, or rounds other values in their place, can miss the bound.
Values may be sent and summed in bfloat16 or wider, within the bound.
A program may use at most 128 MiB of HBM per device.

v0:
```python
import jax
import jax.numpy as jnp
from jax import lax
from jax.sharding import PartitionSpec as P

HD = 64
BS = 128


def with_halo(cells, sides, width):
    for axis, dim in sides:
        count = lax.axis_size(axis)
        ends = count - 1
        head = lax.slice_in_dim(cells, 0, width, axis=dim)
        tail = lax.slice_in_dim(cells, cells.shape[dim] - width, cells.shape[dim], axis=dim)
        cells = jnp.concatenate(
            [
                lax.ppermute(tail, axis, [(i, (i + 1) % count) for i in range(ends)]),
                cells,
                lax.ppermute(head, axis, [((i + 1) % count, i) for i in range(ends)]),
            ],
            axis=dim,
        )
    return cells


def shifted(x, axis, by):
    count = lax.axis_size(axis)
    pairs = [(i, i + by) for i in range(count) if 0 <= i + by < count]
    return lax.ppermute(x, axis, pairs)


def head_scores(query_block, key_block, factor):
    return (
        jnp.einsum("qhd,khd->hqk", query_block, key_block, preferred_element_type=jnp.float32)
        * factor
    )


def masked_scores(query_block, key_block, usable, factor):
    key_mask = jnp.repeat(usable, key_block.shape[0] // usable.shape[0])
    return jnp.where(key_mask[None, None, :], head_scores(query_block, key_block, factor), -1e30)


def padded_forward(query_block, key_block, value_block, usable, factor):
    scores = masked_scores(query_block, key_block, usable, factor)
    highest = jnp.max(scores, axis=2)
    log_total = highest + jnp.log(jnp.sum(jnp.exp(scores - highest[:, :, None]), axis=2))
    soft_weights = jnp.exp(scores - log_total[:, :, None]).astype(jnp.bfloat16)
    attended = jnp.einsum(
        "hqk,khd->qhd", soft_weights, value_block, preferred_element_type=jnp.float32
    )
    return (attended.astype(jnp.bfloat16), log_total)


def pair_backward(
    query_block, grad_block, log_total, dot_block, key_block, value_block, usable, factor
):
    scores = masked_scores(query_block, key_block, usable, factor)
    soft_full = jnp.exp(scores - log_total[:, :, None])
    grad_weights = jnp.einsum(
        "qhd,khd->hqk", grad_block, value_block, preferred_element_type=jnp.float32
    )
    grad_scores = (soft_full * (grad_weights - dot_block[:, :, None])).astype(jnp.bfloat16)
    grad_query = (
        jnp.einsum("hqk,khd->qhd", grad_scores, key_block, preferred_element_type=jnp.float32)
        * factor
    )
    grad_key = (
        jnp.einsum("hqk,qhd->khd", grad_scores, query_block, preferred_element_type=jnp.float32)
        * factor
    )
    grad_value = jnp.einsum(
        "hqk,qhd->khd",
        soft_full.astype(jnp.bfloat16),
        grad_block,
        preferred_element_type=jnp.float32,
    )
    return (grad_query, grad_key, grad_value)


def body(query_rows, key_rows, value_rows, out_grad, out_weight, neighbours, counts):
    row_count, col_count = query_rows.shape
    head_count = col_count // HD
    blocks = row_count // BS
    extent = 3 * blocks
    slot_total = neighbours.shape[1]
    block_total = counts.shape[0]
    factor = HD ** (-0.5)
    ctx_index = lax.axis_index("ctx")
    offset = (ctx_index - 1) * blocks
    packed = jnp.concatenate([key_rows, value_rows], axis=1)
    window = with_halo(packed, (("ctx", 0),), row_count)
    window = window.reshape(extent, BS, 2 * col_count)
    slot_ids = jnp.arange(slot_total, dtype=jnp.int32)
    query_blocks = query_rows.reshape(blocks, BS, head_count, HD)

    def fetch_all(places):
        picked = window[places]
        key_block = picked[:, :, :col_count].reshape(slot_total * BS, head_count, HD)
        value_block = picked[:, :, col_count:].reshape(slot_total * BS, head_count, HD)
        return (key_block, value_block)

    def slot_table(block_id):
        inside = (block_id >= 0) & (block_id < block_total)
        clamped = jnp.clip(block_id, 0, block_total - 1)
        relative = neighbours[clamped] - offset
        places = jnp.clip(relative, 0, extent - 1)
        active = jnp.where(inside, counts[clamped], 0)
        return (relative, places, active)

    def forward_block(block_index):
        relative, places, active = slot_table(ctx_index * blocks + block_index)
        query_block = query_blocks[block_index]
        key_block, value_block = fetch_all(places)
        return padded_forward(query_block, key_block, value_block, slot_ids < active, factor)

    attended_blocks, log_totals = lax.map(forward_block, jnp.arange(blocks, dtype=jnp.int32))
    attended = attended_blocks.reshape(row_count, col_count)
    shard_piece = lax.all_gather(out_grad, "head", axis=1, tiled=True)
    grad_sum = jnp.einsum("ro,jo->rj", shard_piece, out_weight, preferred_element_type=jnp.float32)
    product = jnp.einsum("rj,ro->jo", attended, shard_piece, preferred_element_type=jnp.float32)
    weight_sum = product
    grad_sum, weight_sum = (grad_sum, weight_sum)
    node_count = row_count * lax.axis_size("ctx")
    weight_grad = lax.psum(weight_sum, "ctx") * node_count ** (-0.5)
    grad_attended = grad_sum.astype(jnp.bfloat16)
    grad_blocks = grad_attended.reshape(blocks, BS, head_count, HD)
    row_dots = jnp.sum(
        grad_blocks.astype(jnp.float32) * attended_blocks.astype(jnp.float32), axis=3
    ).transpose(0, 2, 1)

    def sweep_step(totals, block_index):
        relative, places, active = slot_table(ctx_index * blocks + block_index)
        query_block = query_blocks[block_index]
        grad_block = grad_blocks[block_index]
        log_total = log_totals[block_index]
        dot_block = row_dots[block_index]
        key_block, value_block = fetch_all(places)
        grad_query, grad_key, grad_value = pair_backward(
            query_block,
            grad_block,
            log_total,
            dot_block,
            key_block,
            value_block,
            slot_ids < active,
            factor,
        )
        update = jnp.concatenate(
            [
                grad_key.reshape(slot_total, BS, col_count),
                grad_value.reshape(slot_total, BS, col_count),
            ],
            axis=2,
        )
        totals = totals.at[places].add(jnp.where((slot_ids < active)[:, None, None], update, 0.0))
        return (totals, grad_query.astype(jnp.bfloat16))

    blank_totals = jnp.zeros((extent, BS, 2 * col_count), jnp.float32)
    totals, grad_queries = lax.scan(sweep_step, blank_totals, jnp.arange(blocks, dtype=jnp.int32))
    middle = totals[blocks : 2 * blocks]
    from_right = shifted(totals[:blocks], "ctx", -1)
    from_left = shifted(totals[2 * blocks :], "ctx", 1)
    combined = middle + from_right + from_left
    query_grad = grad_queries.reshape(row_count, col_count)
    key_grad = combined[:, :, :col_count].reshape(row_count, col_count).astype(jnp.bfloat16)
    value_grad = combined[:, :, col_count:].reshape(row_count, col_count).astype(jnp.bfloat16)
    return (query_grad, key_grad, value_grad, weight_grad)


def solution(mesh):
    placed = (
        P("ctx", "head"),
        P("ctx", "head"),
        P("ctx", "head"),
        P("ctx", "head"),
        P("head", None),
        P(),
        P(),
    )
    return jax.shard_map(
        body,
        mesh=mesh,
        in_specs=placed,
        out_specs=(P("ctx", "head"), P("ctx", "head"), P("ctx", "head"), P("head", None)),
        check_vma=False,
    )
```

profile of v0, /device:TPU:11, one launch (start us, length us, event | category | flops | bytes accessed | tf_op | source)
XLA Modules:
  0.0 1101.9 jit_solution(16975583214655846279)
XLA Ops:
  22.6 21.2 %all-gather.2.cloned.1.call-done = bf16[1024,1024]{1,0:T(8,128)(2,1)} async-done(((bf16[1024,512]{1,0:T(8,128)(2,1)}), bf16[1024,1024]{1,0:T(8,128)(2,1)}) %all-gather.2.cloned.1.call-update) | async-done | bytes 2097168 | tf_op jit(solution)/shard_map/all_gather | solution.py:120
  48.8 6.0 pad_maximum_fusion
  56.1 244.0 %while.30 = (s32[]{:T(128)}, bf16[8,128,8,64]{1,3,2,0:T(8,128)(2,1)}, f32[8,8,128]{2,1,0:T(8,128)S(1)}, s32[8]{0:T(128)S(1)}, s32[]{:T(128)}, /*index=5*/s32[128...) while((s32[]{:T(128)}, ...), condition=%wide.region_3.4_spmd.clone, body=%wide.region_0.3_spmd.clone.sunk | while | flops 420020288 | bytes 53783068 | solution.py:118
  302.3 6.1 broadcast_in_dim.88
  308.4 633.0 %while.31 = (s32[]{:T(128)}, f32[24,128,1024]{2,1,0:T(8,128)}, bf16[8,128,8,64]{1,3,2,0:T(8,128)(2,1)S(1)}, s32[8]{0:T(128)S(1)}, s32[]{:T(128)}, /*index=5*/s32...) while((s32[]{:T(128)}, f32[24,128,1024]{2,1,0:T(8,128)}, ...), condition=%wide.region_7.8_spmd.clone, body=%wide.region_5.7_spmd.clone.sunk | while | flops 1027998784 | bytes 128095352 | solution.py:161
  358.9 7.4 maximum_select_fusion.2
  366.3 8.3 copy.91
  374.5 12.9 %scatter_fusion = f32[24,128,1024]{2,1,0:T(8,128)} fusion(f32[24,128,1024]{2,1,0:T(8,128)} %get-tuple-element.729, s32[12]{0:T(128)S(1)} %fusion.101, f32[12,128,1024]{2,1,0:T(8,128)} %copy.91), kind=kCustom, calls=%fused_computation.2.clone.clone.1 | custom fusion | flops 1572864 | bytes 18874416 | tf_op jit(solution)/shard_map/while/body/eval_jaxpr/scatter-add | solution.py:157
  437.9 7.4 maximum_select_fusion.2
  445.2 8.3 copy.91
  453.5 12.9 %scatter_fusion = f32[24,128,1024]{2,1,0:T(8,128)} fusion(f32[24,128,1024]{2,1,0:T(8,128)} %get-tuple-element.729, s32[12]{0:T(128)S(1)} %fusion.101, f32[12,128,1024]{2,1,0:T(8,128)} %copy.91), kind=kCustom, calls=%fused_computation.2.clone.clone.1 | custom fusion | flops 1572864 | bytes 18874416 | tf_op jit(solution)/shard_map/while/body/eval_jaxpr/scatter-add | solution.py:157
  516.9 7.4 maximum_select_fusion.2
  524.3 8.3 copy.91
  532.5 13.0 %scatter_fusion = f32[24,128,1024]{2,1,0:T(8,128)} fusion(f32[24,128,1024]{2,1,0:T(8,128)} %get-tuple-element.729, s32[12]{0:T(128)S(1)} %fusion.101, f32[12,128,1024]{2,1,0:T(8,128)} %copy.91), kind=kCustom, calls=%fused_computation.2.clone.clone.1 | custom fusion | flops 1572864 | bytes 18874416 | tf_op jit(solution)/shard_map/while/body/eval_jaxpr/scatter-add | solution.py:157
  596.0 7.4 maximum_select_fusion.2
  603.4 8.3 copy.91
  611.7 13.2 %scatter_fusion = f32[24,128,1024]{2,1,0:T(8,128)} fusion(f32[24,128,1024]{2,1,0:T(8,128)} %get-tuple-element.729, s32[12]{0:T(128)S(1)} %fusion.101, f32[12,128,1024]{2,1,0:T(8,128)} %copy.91), kind=kCustom, calls=%fused_computation.2.clone.clone.1 | custom fusion | flops 1572864 | bytes 18874416 | tf_op jit(solution)/shard_map/while/body/eval_jaxpr/scatter-add | solution.py:157
  675.3 7.4 maximum_select_fusion.2
  682.7 8.3 copy.91
  691.0 13.0 %scatter_fusion = f32[24,128,1024]{2,1,0:T(8,128)} fusion(f32[24,128,1024]{2,1,0:T(8,128)} %get-tuple-element.729, s32[12]{0:T(128)S(1)} %fusion.101, f32[12,128,1024]{2,1,0:T(8,128)} %copy.91), kind=kCustom, calls=%fused_computation.2.clone.clone.1 | custom fusion | flops 1572864 | bytes 18874416 | tf_op jit(solution)/shard_map/while/body/eval_jaxpr/scatter-add | solution.py:157
  754.5 7.4 maximum_select_fusion.2
  761.8 8.3 copy.91
  770.1 12.7 %scatter_fusion = f32[24,128,1024]{2,1,0:T(8,128)} fusion(f32[24,128,1024]{2,1,0:T(8,128)} %get-tuple-element.729, s32[12]{0:T(128)S(1)} %fusion.101, f32[12,128,1024]{2,1,0:T(8,128)} %copy.91), kind=kCustom, calls=%fused_computation.2.clone.clone.1 | custom fusion | flops 1572864 | bytes 18874416 | tf_op jit(solution)/shard_map/while/body/eval_jaxpr/scatter-add | solution.py:157
  833.3 7.4 maximum_select_fusion.2
  840.7 8.3 copy.91
  848.9 12.7 %scatter_fusion = f32[24,128,1024]{2,1,0:T(8,128)} fusion(f32[24,128,1024]{2,1,0:T(8,128)} %get-tuple-element.729, s32[12]{0:T(128)S(1)} %fusion.101, f32[12,128,1024]{2,1,0:T(8,128)} %copy.91), kind=kCustom, calls=%fused_computation.2.clone.clone.1 | custom fusion | flops 1572864 | bytes 18874416 | tf_op jit(solution)/shard_map/while/body/eval_jaxpr/scatter-add | solution.py:157
  912.1 7.4 maximum_select_fusion.2
  919.5 8.3 copy.91
  927.8 13.7 %scatter_fusion = f32[24,128,1024]{2,1,0:T(8,128)} fusion(f32[24,128,1024]{2,1,0:T(8,128)} %get-tuple-element.729, s32[12]{0:T(128)S(1)} %fusion.101, f32[12,128,1024]{2,1,0:T(8,128)} %copy.91), kind=kCustom, calls=%fused_computation.2.clone.clone.1 | custom fusion | flops 1572864 | bytes 18874416 | tf_op jit(solution)/shard_map/while/body/eval_jaxpr/scatter-add | solution.py:157
  942.4 8.5 fusion.52
  950.9 19.7 %collective-permute-start.2 = (f32[8,128,1024]{2,1,0:T(8,128)}, f32[8,128,1024]{2,1,0:T(8,128)}, u32[]{:S(2)}, u32[]{:S(2)}) collective-permute-start(f32[8,128,1024]{2,1,0:T(8,128)} %get-tuple-element.505), channel_id=1, source_target_pairs={{2,0},{4,2},{6,4},{8,6},{10,8},{12,10},{14,12},{16,14},{18,16},{20... | collective-permute-start | bytes 12582920 | tf_op jit(solution)/shard_map/ppermute | solution.py:30
  979.4 105.0 %all-reduce.2.cloned.1.call-done = f32[512,1024]{1,0:T(8,128)} async-done(((f32[512,1024]{1,0:T(8,128)}), f32[512,1024]{1,0:T(8,128)}) %all-reduce.2.cloned.1.call-update) | async-done | bytes 2097168 | tf_op jit(solution)/shard_map/psum | solution.py:126
  (379 shorter events, 638.8 us)
Async XLA Ops:
  7.2 36.7 %copy-start = (bf16[512,1024]{1,0:T(8,128)(2,1)S(1)}, bf16[512,1024]{1,0:T(8,128)(2,1)}, u32[]{:S(2)}) copy-start(bf16[512,1024]{1,0:T(8,128)(2,1)} %param.15) | copy-start | bytes 3145732
  7.2 3.1 copy-start.7
  7.2 10.6 copy-start.8
  7.2 36.7 %all-gather.2.cloned.1.call-start = ((), (), s32[]{:S(2)}) async-start(), calls=%async_computation | async-start | bytes 3145728 | tf_op jit(solution)/shard_map/all_gather | solution.py:120
  7.9 1076.4 %all-reduce.2.cloned.1.call-start = ((), (), s32[]{:S(2)}) async-start(), calls=%async_computation.1 | async-start | bytes 4194304 | tf_op jit(solution)/shard_map/psum | solution.py:126
  11.3 37.5 %collective-permute-start.1 = (bf16[1024,1024]{1,0:T(8,128)(2,1)}, bf16[1024,1024]{1,0:T(8,128)(2,1)}, u32[]{:S(2)}, u32[]{:S(2)}) collective-permute-start(bf16[1024,1024]{1,0:T(8,128)(2,1)} %constant_dynamic-update-slice_fusion), channel_id=1, source_target_pairs={{2,0},{4,2},{6,4},{8,6},{10,8},{12,10},{14,12},{16,14},{18,16},{20... | collective-permute-start | bytes 6291464 | tf_op jit(solution)/shard_map/ppermute | solution.py:20
  13.9 35.0 %collective-permute-start = (bf16[1024,1024]{1,0:T(8,128)(2,1)}, bf16[1024,1024]{1,0:T(8,128)(2,1)}, u32[]{:S(2)}, u32[]{:S(2)}) collective-permute-start(bf16[1024,1024]{1,0:T(8,128)(2,1)} %constant_dynamic-update-slice_fusion), channel_id=1, source_target_pairs={{0,2},{2,4},{4,6},{6,8},{8,10},{10,12},{12,14},{14,16},{16,18},{18... | collective-permute-start | bytes 6291464 | tf_op jit(solution)/shard_map/ppermute | solution.py:18
  48.8 7.2 copy-start.10
  82.9 1.4 copy-start.2
  113.4 1.4 copy-start.2
  143.9 1.4 copy-start.2
  174.4 1.4 copy-start.2
  204.9 1.4 copy-start.2
  235.4 1.4 copy-start.2
  265.9 1.4 copy-start.2
  296.4 1.4 copy-start.2
  335.9 2.0 copy-start.3
  414.9 2.0 copy-start.3
  493.9 2.0 copy-start.3
  573.0 2.0 copy-start.3
  652.3 2.0 copy-start.3
  731.5 2.0 copy-start.3
  810.3 2.0 copy-start.3
  889.1 2.0 copy-start.3
  941.4 1.0 copy-start.5
  942.4 30.4 %copy-start.4 = (bf16[8,128,8,64]{1,3,2,0:T(8,128)(2,1)S(1)}, bf16[8,128,8,64]{1,3,2,0:T(8,128)(2,1)}, u32[]{:S(2)}) copy-start(bf16[8,128,8,64]{1,3,2,0:T(8,128)(2,1)} %get-tuple-element.294) | copy-start | bytes 3145732
  942.4 31.1 %copy-start.9 = (bf16[1024,1024]{1,0:T(8,128)(2,1)S(1)}, bf16[1024,1024]{1,0:T(8,128)(2,1)}, u32[]{:S(2)}) copy-start(bf16[1024,1024]{1,0:T(8,128)(2,1)} %all-gather.2.cloned.1.call-done) | copy-start | bytes 6291460
  950.9 136.6 %collective-permute-start.2 = (f32[8,128,1024]{2,1,0:T(8,128)}, f32[8,128,1024]{2,1,0:T(8,128)}, u32[]{:S(2)}, u32[]{:S(2)}) collective-permute-start(f32[8,128,1024]{2,1,0:T(8,128)} %get-tuple-element.505), channel_id=1, source_target_pairs={{2,0},{4,2},{6,4},{8,6},{10,8},{12,10},{14,12},{16,14},{18,16},{20... | collective-permute-start | bytes 12582920 | tf_op jit(solution)/shard_map/ppermute | solution.py:30
  970.6 116.9 %collective-permute-start.3 = (f32[8,128,1024]{2,1,0:T(8,128)}, f32[8,128,1024]{2,1,0:T(8,128)}, u32[]{:S(2)}, u32[]{:S(2)}) collective-permute-start(f32[8,128,1024]{2,1,0:T(8,128)} %get-tuple-element.506), channel_id=1, source_target_pairs={{0,2},{2,4},{4,6},{6,8},{8,10},{10,12},{12,14},{14,16},{16,18},{18... | collective-permute-start | bytes 12582920 | tf_op jit(solution)/shard_map/ppermute | solution.py:30
  973.5 2.6 copy-start.6
  1087.5 7.5 copy-start.1
Sparse Core Ops, SparseCore 0:
  9.6 34.2 all-gather.1
  976.3 108.0 all-reduce.1
where the time goes:
time: 1110 us; the launch traced here: 1100 us
  local copies, waits for them, and re-layouts  534 us (48%)
  other arithmetic  191 us (17%)
  matrix products  154 us (14%)
  waiting for transfers between devices  127 us (11%)
  loops' own time  53 us (5%)
  starting transfers between devices  28.4 us (3%)
  between operations  14.2 us (1%)
    psum x1, waiting for transfers between devices, body(): weight_grad = lax.psum(weight_sum, 'ctx') * node_count ** (-0.5)  105 us
    scatter-add x8, other arithmetic, sweep_step(): totals.at[places]  104 us
    slice x24, local copies, waits for them, and re-layouts, fetch_all(): picked[:, :, col_count:].reshape(slot_total * BS, head_count, HD)  88.2 us
    gather x16, local copies, waits for them, and re-layouts, fetch_all(): picked = window[places]  84.3 us
    slice x24, local copies, waits for them, and re-layouts, fetch_all(): picked[:, :, :col_count].reshape(slot_total * BS, head_count, HD)  81.3 us
    select_n x8, local copies, waits for them, and re-layouts, sweep_step(): jnp.where((slot_ids < active)[:, None, None], update, 0.0)  66.3 us
    select_n x8, other arithmetic, sweep_step(): jnp.where((slot_ids < active)[:, None, None], update, 0.0)  58.9 us
    reshape x16, local copies, waits for them, and re-layouts, fetch_all(): picked[:, :, col_count:].reshape(slot_total * BS, head_count, HD)  47.5 us
  transfers between devices with their start and end apart: 6, of which 2 were waited for; matrix products, arithmetic and copies ran while one was open for 2% of the time, Pallas kernels for 0%

commit v1 on v0

v1 whole, which is shorter than its diff:
```python
import functools

import jax
import jax.numpy as jnp
from jax import lax
from jax.experimental import pallas as pl
from jax.experimental.pallas import tpu as pltpu
from jax.sharding import PartitionSpec as P

HD = 64
BS = 128
LANES = 2 * HD
STEP = 2
FACTOR = HD ** (-0.5)

NN = (((1,), (0,)), ((), ()))
NT = (((1,), (1,)), ((), ()))


def mm(a, b, dims):
    return lax.dot_general(a, b, dims, preferred_element_type=jnp.float32)


def shifted(x, axis, by):
    count = lax.axis_size(axis)
    pairs = [(i, i + by) for i in range(count) if 0 <= i + by < count]
    return lax.ppermute(x, axis, pairs)


def stacked(rows):
    lane = lax.broadcasted_iota(jnp.int32, rows.shape, 1)
    first = jnp.where(lane < HD, rows, 0.0)
    second = jnp.where(lane >= HD, rows, 0.0)
    return jnp.concatenate([first, second], axis=0).astype(jnp.bfloat16)


def own_parts(both):
    return jnp.concatenate([both[:HD, :BS], both[HD:, BS:]], axis=0)


def fold(values, op):
    return op(values.reshape(values.shape[0] // 8, 8, values.shape[1]), axis=0)


def attention_kernel(
    places,
    active,
    q_ref,
    g_ref,
    k_mid,
    v_mid,
    left_ref,
    right_ref,
    att_ref,
    dq_ref,
    out_left,
    out_mid,
    out_right,
    kw,
    vw,
    kt,
    vt,
    sc,
    dk,
    dv,
    *,
    blocks,
    slots,
    pairs,
):
    block = pl.program_id(0)
    width = pairs * LANES

    @pl.when(block == 0)
    def _():
        dk[...] = jnp.zeros_like(dk)
        dv[...] = jnp.zeros_like(dv)

        def place_block(b, carry):
            rows = pl.ds(pl.multiple_of(b * BS, BS), BS)
            for p in range(pairs):
                cols = slice(p * LANES, (p + 1) * LANES)
                vcols = slice(width + p * LANES, width + (p + 1) * LANES)
                for part, (kr, kc, vr, vc) in enumerate(
                    (
                        (left_ref, cols, left_ref, vcols),
                        (k_mid, cols, v_mid, cols),
                        (right_ref, cols, right_ref, vcols),
                    )
                ):
                    at = part * blocks + b
                    kb = kr[rows, kc]
                    vb = vr[rows, vc]
                    kw[p, at] = kb
                    vw[p, at] = vb
                    kt[p, at] = kb.T
                    vt[p, at] = vb.T
            return carry

        lax.fori_loop(0, blocks, place_block, 0)

    count = active[block]
    trips = (count + STEP - 1) // STEP
    base = block * slots
    chunk = STEP * BS

    q2, g2, gt = [], [], []
    for p in range(pairs):
        cols = slice(p * LANES, (p + 1) * LANES)
        q2.append(stacked(q_ref[:, cols].astype(jnp.float32)))
        g = g_ref[:, cols].astype(jnp.float32)
        g2.append(stacked(g))
        gt.append(g.T)
    qs = [(q * FACTOR).astype(jnp.bfloat16) for q in q2]

    def slot_places(t):
        return [places[base + t * STEP + u] for u in range(STEP)]

    def score_step(t, highest):
        at = slot_places(t)
        highest = list(highest)
        for u in range(STEP):
            used = t * STEP + u < count
            rows = pl.ds(pl.multiple_of(t * chunk + u * BS, BS), BS)
            for p in range(pairs):
                s = mm(kw[p, at[u]], qs[p], NT)
                s = jnp.where(used, s, -1e30)
                sc[p, rows, :] = s
                highest[p] = jnp.maximum(highest[p], fold(s, jnp.max))
        return tuple(highest)

    lowest = jnp.full((8, 2 * BS), -1e30, jnp.float32)
    highest = lax.fori_loop(0, trips, score_step, (lowest,) * pairs)
    highest = [jnp.max(x, axis=0, keepdims=True) for x in highest]

    def exp_step(t, total):
        rows = pl.ds(pl.multiple_of(t * chunk, chunk), chunk)
        total = list(total)
        for p in range(pairs):
            e = jnp.exp(sc[p, rows, :] - highest[p])
            sc[p, rows, :] = e
            total[p] = total[p] + fold(e, jnp.sum)
        return tuple(total)

    total = lax.fori_loop(0, trips, exp_step, (jnp.zeros((8, 2 * BS), jnp.float32),) * pairs)
    inverse = [1.0 / jnp.sum(x, axis=0, keepdims=True) for x in total]

    def sum_step(t, acc):
        at = slot_places(t)
        rows = pl.ds(pl.multiple_of(t * chunk, chunk), chunk)
        acc = list(acc)
        for p in range(pairs):
            w = (sc[p, rows, :] * inverse[p]).astype(jnp.bfloat16)
            v_t = jnp.concatenate([vt[p, a] for a in at], axis=1)
            acc[p] = acc[p] + mm(v_t, w, NN)
        return tuple(acc)

    blank = jnp.zeros((LANES, 2 * BS), jnp.float32)
    acc = lax.fori_loop(0, trips, sum_step, (blank,) * pairs)
    dots = []
    for p in range(pairs):
        cols = slice(p * LANES, (p + 1) * LANES)
        o_t = own_parts(acc[p]).astype(jnp.bfloat16).astype(jnp.float32)
        att_ref[:, cols] = o_t.T.astype(jnp.bfloat16)
        prod = o_t * gt[p]
        dots.append(
            jnp.concatenate(
                [
                    jnp.sum(prod[:HD], axis=0, keepdims=True),
                    jnp.sum(prod[HD:], axis=0, keepdims=True),
                ],
                axis=1,
            )
        )

    def grad_step(t, acc):
        at = slot_places(t)
        acc = list(acc)
        for p in range(pairs):
            ds_all = []
            for u in range(STEP):
                rows = pl.ds(pl.multiple_of(t * chunk + u * BS, BS), BS)
                w = sc[p, rows, :] * inverse[p]
                dp = mm(vw[p, at[u]], g2[p], NT)
                ds = (w * (dp - dots[p])).astype(jnp.bfloat16)
                dv[p, at[u]] += mm(w.astype(jnp.bfloat16), g2[p], NN)
                dk[p, at[u]] += mm(ds, q2[p], NN)
                ds_all.append(ds)
            k_t = jnp.concatenate([kt[p, a] for a in at], axis=1)
            acc[p] = acc[p] + mm(k_t, jnp.concatenate(ds_all, axis=0), NN)
        return tuple(acc)

    acc = lax.fori_loop(0, trips, grad_step, (blank,) * pairs)
    for p in range(pairs):
        cols = slice(p * LANES, (p + 1) * LANES)
        dq_ref[:, cols] = (own_parts(acc[p]).T * FACTOR).astype(jnp.bfloat16)

    @pl.when(block == blocks - 1)
    def _():
        def put_block(b, carry):
            rows = pl.ds(pl.multiple_of(b * BS, BS), BS)
            for p in range(pairs):
                cols = slice(p * LANES, (p + 1) * LANES)
                vcols = slice(width + p * LANES, width + (p + 1) * LANES)
                for part, out in enumerate((out_left, out_mid, out_right)):
                    at = part * blocks + b
                    out[rows, cols] = (dk[p, at] * FACTOR).astype(out.dtype)
                    out[rows, vcols] = dv[p, at].astype(out.dtype)
            return carry

        lax.fori_loop(0, blocks, put_block, 0)


def group_attention(places, active, queries, grads, keys, values, left, right, group, pairs):
    rows = queries.shape[0]
    blocks = rows // BS
    slots = places.shape[0] // blocks
    width = pairs * LANES
    tile = pl.BlockSpec((BS, width), lambda i, *_: (i, group))
    whole = pl.BlockSpec((rows, width), lambda i, *_: (0, group))
    out_tile = pl.BlockSpec((BS, width), lambda i, *_: (i, 0))
    packed = pl.BlockSpec((rows, 2 * width), lambda i, *_: (0, 0))
    window = (pairs, 3 * blocks, BS, LANES)
    padded = (slots + STEP - 1) // STEP * STEP
    return pl.pallas_call(
        functools.partial(attention_kernel, blocks=blocks, slots=slots, pairs=pairs),
        grid_spec=pltpu.PrefetchScalarGridSpec(
            num_scalar_prefetch=2,
            grid=(blocks,),
            in_specs=[tile, tile, whole, whole, packed, packed],
            out_specs=[out_tile, out_tile, packed, packed, packed],
            scratch_shapes=[
                pltpu.VMEM(window, jnp.bfloat16),
                pltpu.VMEM(window, jnp.bfloat16),
                pltpu.VMEM(window, jnp.bfloat16),
                pltpu.VMEM(window, jnp.bfloat16),
                pltpu.VMEM((pairs, padded * BS, 2 * BS), jnp.float32),
                pltpu.VMEM(window, jnp.float32),
                pltpu.VMEM(window, jnp.float32),
            ],
        ),
        out_shape=[
            jax.ShapeDtypeStruct((rows, width), jnp.bfloat16),
            jax.ShapeDtypeStruct((rows, width), jnp.bfloat16),
            jax.ShapeDtypeStruct((rows, 2 * width), jnp.bfloat16),
            jax.ShapeDtypeStruct((rows, 2 * width), jnp.float32),
            jax.ShapeDtypeStruct((rows, 2 * width), jnp.bfloat16),
        ],
        compiler_params=pltpu.CompilerParams(
            dimension_semantics=("arbitrary",), vmem_limit_bytes=48 * 1024 * 1024
        ),
        cost_estimate=pl.CostEstimate(
            flops=7 * 2 * 2 * blocks * slots * pairs * BS * BS * LANES,
            bytes_accessed=rows * width * 32,
            transcendentals=2 * blocks * slots * pairs * BS * BS,
        ),
    )(places, active, queries, grads, keys, values, left, right)


def body(query_rows, key_rows, value_rows, out_grad, out_weight, neighbours, counts):
    row_count, col_count = query_rows.shape
    blocks = row_count // BS
    slots = neighbours.shape[1]
    pair_total = col_count // LANES
    pairs = 2 if pair_total % 2 == 0 else 1
    groups = pair_total // pairs
    width = pairs * LANES
    ctx_index = lax.axis_index("ctx")
    head_index = lax.axis_index("head")

    halos = []
    for g in range(groups):
        cols = slice(g * width, (g + 1) * width)
        packed = jnp.concatenate([key_rows[:, cols], value_rows[:, cols]], axis=1)
        halos.append((shifted(packed, "ctx", 1), shifted(packed, "ctx", -1)))

    if lax.axis_size("head") == 2:
        other = lax.ppermute(out_grad, "head", [(0, 1), (1, 0)])
        first = jnp.where(head_index == 0, out_grad, other)
        second = jnp.where(head_index == 0, other, out_grad)
        cotangent = jnp.concatenate([first, second], axis=1)
    else:
        cotangent = lax.all_gather(out_grad, "head", axis=1, tiled=True)
    grad_attended = jnp.einsum(
        "ro,jo->rj", cotangent, out_weight, preferred_element_type=jnp.float32
    ).astype(jnp.bfloat16)

    first_block = ctx_index * blocks
    listed = lax.dynamic_slice_in_dim(neighbours, first_block, blocks, axis=0)
    active = lax.dynamic_slice_in_dim(counts, first_block, blocks, axis=0)
    places = jnp.clip(listed - (first_block - blocks), 0, 3 * blocks - 1)
    if slots % STEP:
        places = jnp.concatenate([places, places[:, :1]], axis=1)
    places = places.reshape(-1)
    scale = (row_count * lax.axis_size("ctx")) ** (-0.5)

    query_parts, key_parts, value_parts, weight_parts = [], [], [], []
    for g in range(groups):
        left, right = halos[g]
        attended, dq, to_left, middle, to_right = group_attention(
            places,
            active,
            query_rows,
            grad_attended,
            key_rows,
            value_rows,
            left,
            right,
            g,
            pairs,
        )
        product = jnp.einsum("rj,ro->jo", attended, cotangent, preferred_element_type=jnp.float32)
        weight_parts.append(lax.psum(product, "ctx") * scale)
        from_right = shifted(to_left, "ctx", -1).astype(jnp.float32)
        from_left = shifted(to_right, "ctx", 1).astype(jnp.float32)
        combined = (middle + from_right + from_left).astype(jnp.bfloat16)
        query_parts.append(dq)
        key_parts.append(combined[:, :width])
        value_parts.append(combined[:, width:])
    return (
        jnp.concatenate(query_parts, axis=1),
        jnp.concatenate(key_parts, axis=1),
        jnp.concatenate(value_parts, axis=1),
        jnp.concatenate(weight_parts, axis=0),
    )


def solution(mesh):
    placed = (
        P("ctx", "head"),
        P("ctx", "head"),
        P("ctx", "head"),
        P("ctx", "head"),
        P("head", None),
        P(),
        P(),
    )
    return jax.shard_map(
        body,
        mesh=mesh,
        in_specs=placed,
        out_specs=(P("ctx", "head"), P("ctx", "head"), P("ctx", "head"), P("head", None)),
        check_vma=False,
    )
```

time: 1110 us -> 261 us (0.24)
  local copies, waits for them, and re-layouts: 534 us -> 2.82 us
  other arithmetic: 191 us -> 12.3 us
  matrix products: 154 us -> 4.72 us
  Pallas kernels: 0 us -> 79.8 us
  loops' own time: 53 us -> 0 us
  waiting for transfers between devices: 127 us -> 105 us
    slice x50 -> x3, local copies, waits for them, and re-layouts: 179 us -> 1.79 us  [the longest x1 1.65 us: body(): packed = jnp.concatenate([key_rows[:, cols], value_rows[:, cols]], axis=1)]
    reshape x49 -> x1, local copies, waits for them, and re-layouts: 164 us -> 0.08 us  [body(): places = places.reshape(-1)]
    dot_general x58 -> x3, matrix products: 154 us -> 4.72 us  [the longest x2 3.44 us: body(): jnp.einsum('rj,ro->jo', attended, cotangent, preferred_element_type=jnp.f...]
    scatter-add x8 -> x0, other arithmetic: 104 us -> none  [sweep_step(): totals.at[places]]
    gather x16 -> x0, local copies, waits for them, and re-layouts: 84.3 us -> none  [fetch_all(): picked = window[places]]
    pallas_call x0 -> x2, Pallas kernels: none -> 79.8 us  [group_attention(): pl.pallas_call(functools.partial(attention_kernel, blocks=blocks, slots=s...]
    select_n x8 -> x0, local copies, waits for them, and re-layouts: 66.3 us -> none  [sweep_step(): jnp.where((slot_ids < active)[:, None, None], update, 0.0)]
    select_n x24 -> x1, other arithmetic: 59.1 us -> 0.14 us  [body(): first = jnp.where(head_index == 0, out_grad, other)]
  transfers between devices with their start and end apart: 6 -> 10, of which waited for: 2 -> 2; matrix products, arithmetic and copies ran while one was open for 2% -> 5% of each run, Pallas kernels for 0% -> 31%
where the time goes in v1:
time: 261 us; the launch traced here: 257 us
  waiting for transfers between devices  105 us (40%)
  Pallas kernels  79.8 us (31%)
  starting transfers between devices  37.7 us (14%)
  between operations  14.3 us (5%)
  other arithmetic  12.3 us (5%)
  matrix products  4.72 us (2%)
  local copies, waits for them, and re-layouts  2.82 us (1%)
    psum x1, waiting for transfers between devices, body(): weight_parts.append(lax.psum(product, 'ctx') * scale)  98.8 us
    pallas_call x2, Pallas kernels, group_attention(): pl.pallas_call(functools.partial(attention_kernel, blocks=blocks, slots=s...  79.8 us
    ppermute x8, starting transfers between devices, shifted(): return lax.ppermute(x, axis, pairs)  36.3 us
    ppermute x1, waiting for transfers between devices, body(): other = lax.ppermute(out_grad, 'head', [(0, 1), (1, 0)])  6.03 us
  transfers between devices with their start and end apart: 10, of which 2 were waited for; matrix products, arithmetic and copies ran while one was open for 5% of the time, Pallas kernels for 31%

profile of v1, /device:TPU:11, one launch (start us, length us, event | category | flops | bytes accessed | tf_op | source)
XLA Modules:
  0.0 256.5 jit_solution(10551095610507939088)
XLA Ops:
  7.2 1.3 collective-permute-start
  8.5 1.7 fusion.7
  10.2 1.1 pad_maximum_fusion.2
  11.3 2.9 %collective-permute-start.2 = (bf16[1024,512]{1,0:T(8,128)(2,1)}, bf16[1024,512]{1,0:T(8,128)(2,1)}, u32[]{:S(2)}, u32[]{:S(2)}) collective-permute-start(bf16[1024,512]{1,0:T(8,128)(2,1)} %pad_maximum_fusion.2), channel_id=1, source_target_pairs={{2,0},{4,2},{6,4},{8,6},{10,8},{12,10},{14,12},{16,14},{18,16},{20... | collective-permute-start | bytes 3145736 | tf_op jit(solution)/shard_map/ppermute | solution.py:27
  14.1 3.6 %collective-permute-start.1 = (bf16[1024,512]{1,0:T(8,128)(2,1)}, bf16[1024,512]{1,0:T(8,128)(2,1)}, u32[]{:S(2)}, u32[]{:S(2)}) collective-permute-start(bf16[1024,512]{1,0:T(8,128)(2,1)} %pad_maximum_fusion.2), channel_id=1, source_target_pairs={{0,2},{2,4},{4,6},{6,8},{8,10},{10,12},{12,14},{14,16},{16,18},{18... | collective-permute-start | bytes 3145736 | tf_op jit(solution)/shard_map/ppermute | solution.py:27
  17.7 1.1 pad_maximum_fusion.3
  18.8 1.9 collective-permute-start.4
  20.7 4.5 %collective-permute-start.3 = (bf16[1024,512]{1,0:T(8,128)(2,1)}, bf16[1024,512]{1,0:T(8,128)(2,1)}, u32[]{:S(2)}, u32[]{:S(2)}) collective-permute-start(bf16[1024,512]{1,0:T(8,128)(2,1)} %pad_maximum_fusion.3), channel_id=1, source_target_pairs={{0,2},{2,4},{4,6},{6,8},{8,10},{10,12},{12,14},{14,16},{16,18},{18... | collective-permute-start | bytes 3145736 | tf_op jit(solution)/shard_map/ppermute | solution.py:27
  25.3 0.1 dynamic_slice.7.active
  25.4 0.1 copy.13
  25.5 0.1 reshape.11.places
  25.6 6.0 %collective-permute-done = bf16[1024,512]{1,0:T(8,128)(2,1)S(1)} collective-permute-done((bf16[1024,512]{1,0:T(8,128)(2,1)}, bf16[1024,512]{1,0:T(8,128)(2,1)S(1)}, u32[]{:S(2)}, u32[]{:S(2)}) %collective-permute-start) | collective-permute-done | bytes 1048608 | tf_op jit(solution)/shard_map/ppermute | solution.py:278
  31.6 0.1 broadcast_select_fusion.1
  31.8 1.3 convolution_convert_fusion.g_ref
  33.1 40.2 %shard_map.102 = (bf16[1024,256]{1,0:T(8,128)(2,1)S(1)}, bf16[1024,256]{1,0:T(8,128)(2,1)S(1)}, bf16[1024,512]{1,0:T(8,128)(2,1)}, f32[1024,512]{1,0:T(8,128)}, bf16[1024,512]{1,0:T(8,128)(2,1)}) custom-call(s32[96]{0:T(128)S(1)} %reshape.11.places, s32[8]{0:T(128)S(1)} %dynamic_slice.7.active, bf16[1024,512]{1,0:T(8,128)(2,1)S(1)} %copy-done.1, ...), custom_call_target="tpu_custom_call" | custom-call | flops 11274289152 | bytes 8388608 | tf_op jit(solution)/shard_map/pallas_call | solution.py:225
  73.4 8.2 %collective-permute-start.5 = (bf16[1024,512]{1,0:T(8,128)(2,1)}, bf16[1024,512]{1,0:T(8,128)(2,1)}, u32[]{:S(2)}, u32[]{:S(2)}) collective-permute-start(bf16[1024,512]{1,0:T(8,128)(2,1)} %get-tuple-element.17), channel_id=1, source_target_pairs={{2,0},{4,2},{6,4},{8,6},{10,8},{12,10},{14,12},{16,14},{18,16},{20... | collective-permute-start | bytes 3145736 | tf_op jit(solution)/shard_map/ppermute | solution.py:27
  81.6 1.9 collective-permute-start.6
  83.5 39.5 %shard_map.103 = (bf16[1024,256]{1,0:T(8,128)(2,1)S(1)}, bf16[1024,256]{1,0:T(8,128)(2,1)S(1)}, bf16[1024,512]{1,0:T(8,128)(2,1)S(1)}, f32[1024,512]{1,0:T(8,128)}, bf16[1024,512]{1,0:T(8,128)(2,1)S(1)}) custom-call(s32[96]{0:T(128)S(1)} %reshape.11.places, s32[8]{0:T(128)S(1)} %dynamic_slice.7.active, bf16[1024,512]{1,0:T(8,128)(2,1)S(1)} %copy-done.1, ...), custom_call_target="tpu_custom_call" | custom-call | flops 11274289152 | bytes 8388608 | tf_op jit(solution)/shard_map/pallas_call | solution.py:225
  123.0 1.7 fusion.1
  124.8 1.7 fusion
  126.5 2.1 collective-permute-start.7
  128.6 11.3 %collective-permute-start.8 = (bf16[1024,512]{1,0:T(8,128)(2,1)S(1)}, bf16[1024,512]{1,0:T(8,128)(2,1)}, u32[]{:S(2)}, u32[]{:S(2)}) collective-permute-start(bf16[1024,512]{1,0:T(8,128)(2,1)S(1)} %get-tuple-element.21), channel_id=1, source_target_pairs={{0,2},{2,4},{4,6},{6,8},{8,10},{10,12},{12,14},{14,16},{16,18},{18... | collective-permute-start | bytes 3145736 | tf_op jit(solution)/shard_map/ppermute | solution.py:27
  139.9 1.1 pad_maximum_fusion.4
  140.9 2.0 add_convert_fusion.1
  143.0 98.8 %all-reduce.3.cloned.1.call-done = (f32[256,1024]{1,0:T(8,128)}, f32[256,1024]{1,0:T(8,128)}) async-done(((f32[256,1024]{1,0:T(8,128)}, f32[256,1024]{1,0:T(8,128)}), (f32[256,1024]{1,0:T(8,128)}, f32[256,1024]{1,0:T(8,128)})) %all-reduce.3.cloned.1.call-update) | async-done | bytes 2097168 | tf_op jit(solution)/shard_map/psum | solution.py:313
  241.8 1.4 broadcast_multiply_fusion
  243.3 0.1 copy-done.6
  243.5 0.6 copy-done.3
  244.1 2.0 add_convert_fusion
  246.1 1.5 pad_maximum_fusion.1
  247.6 1.1 pad_maximum_fusion.6
  248.6 1.1 pad_maximum_fusion.5
  (31 shorter events, 0.4 us)
Async XLA Ops:
  7.2 24.6 %copy-start = (bf16[512,1024]{1,0:T(8,128)(2,1)S(1)}, bf16[512,1024]{1,0:T(8,128)(2,1)}, u32[]{:S(2)}) copy-start(bf16[512,1024]{1,0:T(8,128)(2,1)} %param.11) | copy-start | bytes 3145732
  7.2 234.6 %all-reduce.3.cloned.1.call-start = ((), (), s32[]{:S(2)}) async-start(), calls=%async_computation | async-start | bytes 4194304 | tf_op jit(solution)/shard_map/psum | solution.py:313
  7.2 24.4 %collective-permute-start = (bf16[1024,512]{1,0:T(8,128)(2,1)}, bf16[1024,512]{1,0:T(8,128)(2,1)S(1)}, u32[]{:S(2)}, u32[]{:S(2)}) collective-permute-start(bf16[1024,512]{1,0:T(8,128)(2,1)} %param.10), channel_id=1, source_target_pairs={{0,1},{1,0},{2,3},{3,2},{4,5},{5,4},{6,7},{7,6},{8,9},{9,8},{10,11... | collective-permute-start | bytes 3145736 | tf_op jit(solution)/shard_map/ppermute | solution.py:278
  10.2 15.1 %copy-start.8 = (s32[128]{0:T(128)S(1)}, s32[128]{0:T(128)}, u32[]{:S(2)}) copy-start(s32[128]{0:T(128)} %param.13) | copy-start | bytes 1540
  10.2 15.2 %copy-start.7 = (s32[128,12]{0,1:T(8,128)S(1)}, s32[128,12]{0,1:T(8,128)}, u32[]{:S(2)}) copy-start(s32[128,12]{0,1:T(8,128)} %param.12) | copy-start | bytes 18436
  10.2 21.4 %copy-start.5 = (bf16[1024,512]{1,0:T(8,128)(2,1)S(1)}, bf16[1024,512]{1,0:T(8,128)(2,1)}, u32[]{:S(2)}) copy-start(bf16[1024,512]{1,0:T(8,128)(2,1)} %param.10) | copy-start | bytes 3145732
  11.3 21.8 %collective-permute-start.2 = (bf16[1024,512]{1,0:T(8,128)(2,1)}, bf16[1024,512]{1,0:T(8,128)(2,1)}, u32[]{:S(2)}, u32[]{:S(2)}) collective-permute-start(bf16[1024,512]{1,0:T(8,128)(2,1)} %pad_maximum_fusion.2), channel_id=1, source_target_pairs={{2,0},{4,2},{6,4},{8,6},{10,8},{12,10},{14,12},{16,14},{18,16},{20... | collective-permute-start | bytes 3145736 | tf_op jit(solution)/shard_map/ppermute | solution.py:27
  14.1 19.0 %collective-permute-start.1 = (bf16[1024,512]{1,0:T(8,128)(2,1)}, bf16[1024,512]{1,0:T(8,128)(2,1)}, u32[]{:S(2)}, u32[]{:S(2)}) collective-permute-start(bf16[1024,512]{1,0:T(8,128)(2,1)} %pad_maximum_fusion.2), channel_id=1, source_target_pairs={{0,2},{2,4},{4,6},{6,8},{8,10},{10,12},{12,14},{14,16},{16,18},{18... | collective-permute-start | bytes 3145736 | tf_op jit(solution)/shard_map/ppermute | solution.py:27
  18.8 64.7 %collective-permute-start.4 = (bf16[1024,512]{1,0:T(8,128)(2,1)}, bf16[1024,512]{1,0:T(8,128)(2,1)}, u32[]{:S(2)}, u32[]{:S(2)}) collective-permute-start(bf16[1024,512]{1,0:T(8,128)(2,1)} %pad_maximum_fusion.3), channel_id=1, source_target_pairs={{2,0},{4,2},{6,4},{8,6},{10,8},{12,10},{14,12},{16,14},{18,16},{20... | collective-permute-start | bytes 3145736 | tf_op jit(solution)/shard_map/ppermute | solution.py:27
  20.7 62.8 %collective-permute-start.3 = (bf16[1024,512]{1,0:T(8,128)(2,1)}, bf16[1024,512]{1,0:T(8,128)(2,1)}, u32[]{:S(2)}, u32[]{:S(2)}) collective-permute-start(bf16[1024,512]{1,0:T(8,128)(2,1)} %pad_maximum_fusion.3), channel_id=1, source_target_pairs={{0,2},{2,4},{4,6},{6,8},{8,10},{10,12},{12,14},{14,16},{16,18},{18... | collective-permute-start | bytes 3145736 | tf_op jit(solution)/shard_map/ppermute | solution.py:27
  31.8 1.3 copy-start.1
  73.4 67.5 %collective-permute-start.5 = (bf16[1024,512]{1,0:T(8,128)(2,1)}, bf16[1024,512]{1,0:T(8,128)(2,1)}, u32[]{:S(2)}, u32[]{:S(2)}) collective-permute-start(bf16[1024,512]{1,0:T(8,128)(2,1)} %get-tuple-element.17), channel_id=1, source_target_pairs={{2,0},{4,2},{6,4},{8,6},{10,8},{12,10},{14,12},{16,14},{18,16},{20... | collective-permute-start | bytes 3145736 | tf_op jit(solution)/shard_map/ppermute | solution.py:27
  81.6 59.3 %collective-permute-start.6 = (bf16[1024,512]{1,0:T(8,128)(2,1)}, bf16[1024,512]{1,0:T(8,128)(2,1)}, u32[]{:S(2)}, u32[]{:S(2)}) collective-permute-start(bf16[1024,512]{1,0:T(8,128)(2,1)} %get-tuple-element.18), channel_id=1, source_target_pairs={{0,2},{2,4},{4,6},{6,8},{8,10},{10,12},{12,14},{14,16},{16,18},{18... | collective-permute-start | bytes 3145736 | tf_op jit(solution)/shard_map/ppermute | solution.py:27
  123.0 1.7 copy-start.2
  126.5 14.4 %copy-start.4 = (f32[1024,512]{1,0:T(8,128)S(1)}, f32[1024,512]{1,0:T(8,128)}, u32[]{:S(2)}) copy-start(f32[1024,512]{1,0:T(8,128)} %get-tuple-element.16) | copy-start | bytes 6291460
  126.5 116.9 %collective-permute-start.7 = (bf16[1024,512]{1,0:T(8,128)(2,1)}, bf16[1024,512]{1,0:T(8,128)(2,1)}, u32[]{:S(2)}, u32[]{:S(2)}) collective-permute-start(bf16[1024,512]{1,0:T(8,128)(2,1)} %copy-done.2), channel_id=1, source_target_pairs={{2,0},{4,2},{6,4},{8,6},{10,8},{12,10},{14,12},{16,14},{18,16},{20... | collective-permute-start | bytes 3145736 | tf_op jit(solution)/shard_map/ppermute | solution.py:27
  128.6 114.9 %collective-permute-start.8 = (bf16[1024,512]{1,0:T(8,128)(2,1)S(1)}, bf16[1024,512]{1,0:T(8,128)(2,1)}, u32[]{:S(2)}, u32[]{:S(2)}) collective-permute-start(bf16[1024,512]{1,0:T(8,128)(2,1)S(1)} %get-tuple-element.21), channel_id=1, source_target_pairs={{0,2},{2,4},{4,6},{6,8},{8,10},{10,12},{12,14},{14,16},{16,18},{18... | collective-permute-start | bytes 3145736 | tf_op jit(solution)/shard_map/ppermute | solution.py:27
  241.8 1.5 copy-start.6
  241.8 2.2 copy-start.3
Sparse Core Ops, SparseCore 0:
  126.6 115.1 all-reduce.2

commit v2 on v1

--- a/solution.py
+++ b/solution.py
@@ -13,12 +13,8 @@
 STEP = 2
 FACTOR = HD ** (-0.5)
 
-NN = (((1,), (0,)), ((), ()))
-NT = (((1,), (1,)), ((), ()))
-
-
-def mm(a, b, dims):
-    return lax.dot_general(a, b, dims, preferred_element_type=jnp.float32)
+def mm(a, b):
+    return jnp.dot(a, b, preferred_element_type=jnp.float32)
 
 
 def shifted(x, axis, by):
@@ -27,19 +23,15 @@
     return lax.ppermute(x, axis, pairs)
 
 
-def stacked(rows):
-    lane = lax.broadcasted_iota(jnp.int32, rows.shape, 1)
-    first = jnp.where(lane < HD, rows, 0.0)
-    second = jnp.where(lane >= HD, rows, 0.0)
-    return jnp.concatenate([first, second], axis=0).astype(jnp.bfloat16)
+def stacked(values, axis):
+    at = lax.broadcasted_iota(jnp.int32, values.shape, axis)
+    first = jnp.where(at < HD, values, 0.0)
+    second = jnp.where(at >= HD, values, 0.0)
+    return jnp.concatenate([first, second], axis=1 - axis).astype(jnp.bfloat16)
 
 
 def own_parts(both):
     return jnp.concatenate([both[:HD, :BS], both[HD:, BS:]], axis=0)
-
-
-def fold(values, op):
-    return op(values.reshape(values.shape[0] // 8, 8, values.shape[1]), axis=0)
 
 
 def attention_kernel(
@@ -60,7 +52,11 @@
     vw,
     kt,
     vt,
+    fixed,
+    fixed_t,
     sc,
+    peak,
+    mass,
     dk,
     dv,
     *,
@@ -104,55 +100,61 @@
     base = block * slots
     chunk = STEP * BS
 
-    q2, g2, gt = [], [], []
+    q_cols, g_cols, gt = [], [], []
     for p in range(pairs):
         cols = slice(p * LANES, (p + 1) * LANES)
-        q2.append(stacked(q_ref[:, cols].astype(jnp.float32)))
+        q = q_ref[:, cols].astype(jnp.float32)
         g = g_ref[:, cols].astype(jnp.float32)
-        g2.append(stacked(g))
         gt.append(g.T)
-    qs = [(q * FACTOR).astype(jnp.bfloat16) for q in q2]
+        fixed[p, 0] = stacked(q, 1)
+        fixed[p, 1] = stacked(g, 1)
+        q_cols.append(stacked(q.T * FACTOR, 0))
+        g_cols.append(stacked(gt[p], 0))
+    for p in range(pairs):
+        fixed_t[p, 0] = q_cols[p]
+        fixed_t[p, 1] = g_cols[p]
 
     def slot_places(t):
         return [places[base + t * STEP + u] for u in range(STEP)]
 
-    def score_step(t, highest):
+    for p in range(pairs):
+        peak[p] = jnp.full(peak.shape[1:], -1e30, jnp.float32)
+        mass[p] = jnp.zeros(mass.shape[1:], jnp.float32)
+
+    def score_step(t, carry):
         at = slot_places(t)
-        highest = list(highest)
-        for u in range(STEP):
-            used = t * STEP + u < count
-            rows = pl.ds(pl.multiple_of(t * chunk + u * BS, BS), BS)
-            for p in range(pairs):
-                s = mm(kw[p, at[u]], qs[p], NT)
-                s = jnp.where(used, s, -1e30)
-                sc[p, rows, :] = s
-                highest[p] = jnp.maximum(highest[p], fold(s, jnp.max))
-        return tuple(highest)
-
-    lowest = jnp.full((8, 2 * BS), -1e30, jnp.float32)
-    highest = lax.fori_loop(0, trips, score_step, (lowest,) * pairs)
-    highest = [jnp.max(x, axis=0, keepdims=True) for x in highest]
-
-    def exp_step(t, total):
-        rows = pl.ds(pl.multiple_of(t * chunk, chunk), chunk)
-        total = list(total)
         for p in range(pairs):
-            e = jnp.exp(sc[p, rows, :] - highest[p])
-            sc[p, rows, :] = e
-            total[p] = total[p] + fold(e, jnp.sum)
-        return tuple(total)
-
-    total = lax.fori_loop(0, trips, exp_step, (jnp.zeros((8, 2 * BS), jnp.float32),) * pairs)
-    inverse = [1.0 / jnp.sum(x, axis=0, keepdims=True) for x in total]
+            both = mm(jnp.concatenate([kw[p, a] for a in at], axis=0), fixed_t[p, 0])
+            for u in range(STEP):
+                slot = t * STEP + u
+                rows = pl.ds(pl.multiple_of(t * chunk + u * BS, BS), BS)
+                s = both[u * BS : (u + 1) * BS]
+                m = jnp.max(s, axis=0, keepdims=True)
+                e = jnp.exp(s - m)
+                sc[p, rows, :] = e
+                peak[p, pl.ds(slot, 1), :] = jnp.where(slot < count, m, -1e30)
+                mass[p, pl.ds(slot, 1), :] = jnp.sum(e, axis=0, keepdims=True)
+        return carry
+
+    lax.fori_loop(0, trips, score_step, 0)
+    for p in range(pairs):
+        ratio = jnp.exp(peak[p] - jnp.max(peak[p], axis=0, keepdims=True))
+        total = jnp.sum(mass[p] * ratio, axis=0, keepdims=True)
+        peak[p] = ratio * (1.0 / total)
+
+    def weights(p, t, u):
+        rows = pl.ds(pl.multiple_of(t * chunk + u * BS, BS), BS)
+        return sc[p, rows, :] * peak[p, pl.ds(t * STEP + u, 1), :]
 
     def sum_step(t, acc):
         at = slot_places(t)
-        rows = pl.ds(pl.multiple_of(t * chunk, chunk), chunk)
         acc = list(acc)
         for p in range(pairs):
-            w = (sc[p, rows, :] * inverse[p]).astype(jnp.bfloat16)
+            w = jnp.concatenate(
+                [weights(p, t, u).astype(jnp.bfloat16) for u in range(STEP)], axis=0
+            )
             v_t = jnp.concatenate([vt[p, a] for a in at], axis=1)
-            acc[p] = acc[p] + mm(v_t, w, NN)
+            acc[p] = acc[p] + mm(v_t, w)
         return tuple(acc)
 
     blank = jnp.zeros((LANES, 2 * BS), jnp.float32)
@@ -177,17 +179,18 @@
         at = slot_places(t)
         acc = list(acc)
         for p in range(pairs):
-            ds_all = []
+            dp = mm(jnp.concatenate([vw[p, a] for a in at], axis=0), fixed_t[p, 1])
+            w = [weights(p, t, u) for u in range(STEP)]
+            ds = [w[u] * (dp[u * BS : (u + 1) * BS] - dots[p]) for u in range(STEP)]
+            w = jnp.concatenate(w, axis=0).astype(jnp.bfloat16)
+            ds = jnp.concatenate(ds, axis=0).astype(jnp.bfloat16)
+            grad_v = mm(w, fixed[p, 1])
+            grad_k = mm(ds, fixed[p, 0])
+            k_t = jnp.concatenate([kt[p, a] for a in at], axis=1)
+            acc[p] = acc[p] + mm(k_t, ds)
             for u in range(STEP):
-                rows = pl.ds(pl.multiple_of(t * chunk + u * BS, BS), BS)
-                w = sc[p, rows, :] * inverse[p]
-                dp = mm(vw[p, at[u]], g2[p], NT)
-                ds = (w * (dp - dots[p])).astype(jnp.bfloat16)
-                dv[p, at[u]] += mm(w.astype(jnp.bfloat16), g2[p], NN)
-                dk[p, at[u]] += mm(ds, q2[p], NN)
-                ds_all.append(ds)
-            k_t = jnp.concatenate([kt[p, a] for a in at], axis=1)
-            acc[p] = acc[p] + mm(k_t, jnp.concatenate(ds_all, axis=0), NN)
+                dv[p, at[u]] += grad_v[u * BS : (u + 1) * BS]
+                dk[p, at[u]] += grad_k[u * BS : (u + 1) * BS]
         return tuple(acc)
 
     acc = lax.fori_loop(0, trips, grad_step, (blank,) * pairs)
@@ -234,7 +237,11 @@
                 pltpu.VMEM(window, jnp.bfloat16),
                 pltpu.VMEM(window, jnp.bfloat16),
                 pltpu.VMEM(window, jnp.bfloat16),
+                pltpu.VMEM((pairs, 2, 2 * BS, LANES), jnp.bfloat16),
+                pltpu.VMEM((pairs, 2, LANES, 2 * BS), jnp.bfloat16),
                 pltpu.VMEM((pairs, padded * BS, 2 * BS), jnp.float32),
+                pltpu.VMEM((pairs, (padded + 7) // 8 * 8, 2 * BS), jnp.float32),
+                pltpu.VMEM((pairs, (padded + 7) // 8 * 8, 2 * BS), jnp.float32),
                 pltpu.VMEM(window, jnp.float32),
                 pltpu.VMEM(window, jnp.float32),
             ],
@@ -257,6 +264,131 @@
     )(places, active, queries, grads, keys, values, left, right)
 
 
+def sum_kernel(*refs, sizes, count):
+    parts, (full, acc, send, *landing, send_sems, recv_sems) = refs[:count], refs[count:]
+    me = lax.axis_index("ctx")
+    stages = []
+    stride = 1
+    for size in sizes:
+        stages.append((size, stride, lax.rem(me // stride, size)))
+        stride *= size
+
+    def peer(stage, away):
+        size, stride, mine = stage
+        other = lax.rem(mine + away, size)
+        return other, me + (other - mine) * stride
+
+    barrier = pltpu.get_barrier_semaphore()
+    greeted = 0
+    for stage in stages:
+        for away in range(1, stage[0]):
+            pl.semaphore_signal(
+                barrier,
+                inc=1,
+                device_id={"ctx": peer(stage, away)[1]},
+                device_id_type=pl.DeviceIdType.MESH,
+            )
+            greeted += 1
+    at = 0
+    for part in parts:
+        acc[pl.ds(at, part.shape[0]), :] = part[...]
+        at += part.shape[0]
+    pl.semaphore_wait(barrier, greeted)
+
+    def copy(src, dst, sem, device):
+        return pltpu.make_async_remote_copy(
+            src_ref=src,
+            dst_ref=dst,
+            send_sem=send_sems.at[sem],
+            recv_sem=recv_sems.at[sem],
+            device_id={"ctx": device},
+            device_id_type=pl.DeviceIdType.MESH,
+        )
+
+    rows = acc.shape[0]
+    start = 0
+    sem = 0
+    pending = []
+    spans = []
+    for stage, land in zip(stages, landing):
+        size, _, mine = stage
+        spans.append((start, rows))
+        piece = rows // size
+        copies = []
+        for away in range(1, size):
+            other, device = peer(stage, away)
+            span = pl.ds(pl.multiple_of(start + other * piece, 16), piece)
+            send[span, :] = acc[span, :].astype(jnp.bfloat16)
+            one = copy(send.at[span, :], land.at[away - 1], sem, device)
+            one.start()
+            copies.append(one)
+            sem += 1
+        start = start + mine * piece
+        own = pl.ds(pl.multiple_of(start, 16), piece)
+        for one in copies:
+            one.wait_recv()
+        total = acc[own, :]
+        for away in range(1, size):
+            total = total + land[away - 1].astype(jnp.float32)
+        acc[own, :] = total
+        rows = piece
+        pending += copies
+    own = pl.ds(pl.multiple_of(start, 16), rows)
+    full[own, :] = acc[own, :].astype(jnp.bfloat16)
+    for stage, (outer, outer_rows) in zip(stages[::-1], spans[::-1]):
+        size, _, mine = stage
+        piece = outer_rows // size
+        span = pl.ds(pl.multiple_of(outer + mine * piece, 16), piece)
+        copies = []
+        for away in range(1, size):
+            one = copy(full.at[span, :], full.at[span, :], sem, peer(stage, away)[1])
+            one.start()
+            copies.append(one)
+            sem += 1
+        for one in copies:
+            one.wait_recv()
+        pending += copies
+    for one in pending:
+        one.wait_send()
+
+
+def summed_over_ctx(parts):
+    count = lax.axis_size("ctx")
+    rows = sum(part.shape[0] for part in parts)
+    cols = parts[0].shape[1]
+    rest = count // 2
+    inner = 2 if rest <= 8 else 8
+    sizes = (2, inner, rest // inner)
+    if rows % (16 * count) or 2 * inner * sizes[2] != count:
+        return lax.psum(jnp.concatenate(parts, axis=0), "ctx")
+    landing = []
+    left = rows
+    for size in sizes:
+        left //= size
+        landing.append(pltpu.VMEM((size - 1, left, cols), jnp.bfloat16))
+    copies = 2 * sum(size - 1 for size in sizes)
+    out = pl.pallas_call(
+        functools.partial(sum_kernel, sizes=sizes, count=len(parts)),
+        out_shape=jax.ShapeDtypeStruct((rows, cols), jnp.bfloat16),
+        in_specs=[pl.BlockSpec(memory_space=pltpu.VMEM)] * len(parts),
+        out_specs=pl.BlockSpec(memory_space=pltpu.VMEM),
+        scratch_shapes=[
+            pltpu.VMEM((rows, cols), jnp.float32),
+            pltpu.VMEM((rows, cols), jnp.bfloat16),
+            *landing,
+            pltpu.SemaphoreType.DMA((copies,)),
+            pltpu.SemaphoreType.DMA((copies,)),
+        ],
+        compiler_params=pltpu.CompilerParams(
+            collective_id=0, has_side_effects=True, vmem_limit_bytes=32 * 1024 * 1024
+        ),
+        cost_estimate=pl.CostEstimate(
+            flops=rows * cols * 4, bytes_accessed=rows * cols * 40, transcendentals=0
+        ),
+    )(*parts)
+    return out.astype(jnp.float32)
+
+
 def body(query_rows, key_rows, value_rows, out_grad, out_weight, neighbours, counts):
     row_count, col_count = query_rows.shape
     blocks = row_count // BS
@@ -310,7 +442,7 @@
             pairs,
         )
         product = jnp.einsum("rj,ro->jo", attended, cotangent, preferred_element_type=jnp.float32)
-        weight_parts.append(lax.psum(product, "ctx") * scale)
+        weight_parts.append(product)
         from_right = shifted(to_left, "ctx", -1).astype(jnp.float32)
         from_left = shifted(to_right, "ctx", 1).astype(jnp.float32)
         combined = (middle + from_right + from_left).astype(jnp.bfloat16)
@@ -321,7 +453,7 @@
         jnp.concatenate(query_parts, axis=1),
         jnp.concatenate(key_parts, axis=1),
         jnp.concatenate(value_parts, axis=1),
-        jnp.concatenate(weight_parts, axis=0),
+        summed_over_ctx(weight_parts) * scale,
     )
 
 

time: 261 us -> 191 us (0.73); the launches traced: 257 us -> 192 us
  waiting for transfers between devices: 105 us -> 6.05 us
  Pallas kernels: 79.8 us -> 126 us
  between operations: 14.3 us -> 0.88 us
  starting transfers between devices: 37.7 us -> 44.2 us
  other arithmetic: 12.3 us -> 7.91 us
    psum x1 -> x0, waiting for transfers between devices: 98.8 us -> none  [body(): weight_parts.append(lax.psum(product, 'ctx') * scale)]
    pallas_call x0 -> x1, Pallas kernels: none -> 43.3 us  [summed_over_ctx(): pl.pallas_call(functools.partial(sum_kernel, sizes=sizes, count=len(parts...]
    ppermute x8, starting transfers between devices: 36.3 us -> 42.9 us  [shifted(): return lax.ppermute(x, axis, pairs)]
    pallas_call x2, Pallas kernels: 79.8 us -> 82.9 us  [group_attention(): pl.pallas_call(functools.partial(attention_kernel, blocks=blocks, slots=s...]
    convert_element_type x2, other arithmetic: 3.96 us -> 0.9 us  [body(): combined = (middle + from_right + from_left).astype(jnp.bfloat16)]
  transfers between devices with their start and end apart: 10 -> 9, of which waited for: 2 -> 1; matrix products, arithmetic and copies ran while one was open for 5% -> 5% of each run, Pallas kernels for 31% -> 66%
where the time goes in v2:
time: 191 us; the launch traced here: 192 us
  Pallas kernels  126 us (66%)
  starting transfers between devices  44.2 us (23%)
  other arithmetic  7.91 us (4%)
  waiting for transfers between devices  6.05 us (3%)
  local copies, waits for them, and re-layouts  4.36 us (2%)
  matrix products  2.73 us (1%)
    pallas_call x2, Pallas kernels, group_attention(): pl.pallas_call(functools.partial(attention_kernel, blocks=blocks, slots=s...  82.9 us
    pallas_call x1, Pallas kernels, summed_over_ctx(): pl.pallas_call(functools.partial(sum_kernel, sizes=sizes, count=len(parts...  43.3 us
    ppermute x8, starting transfers between devices, shifted(): return lax.ppermute(x, axis, pairs)  42.9 us
    ppermute x1, waiting for transfers between devices, body(): other = lax.ppermute(out_grad, 'head', [(0, 1), (1, 0)])  6.03 us
  transfers between devices with their start and end apart: 9, of which 1 were waited for; matrix products, arithmetic and copies ran while one was open for 5% of the time, Pallas kernels for 66%

profile of v2, /device:TPU:11, one launch (start us, length us, event | category | flops | bytes accessed | tf_op | source)
XLA Modules:
  0.0 192.3 jit_solution(12636878895109077149)
XLA Ops:
  0.6 1.3 collective-permute-start
  2.0 1.7 fusion.7
  3.6 1.1 pad_maximum_fusion.1
  4.7 2.9 %collective-permute-start.2 = (bf16[1024,512]{1,0:T(8,128)(2,1)}, bf16[1024,512]{1,0:T(8,128)(2,1)}, u32[]{:S(2)}, u32[]{:S(2)}) collective-permute-start(bf16[1024,512]{1,0:T(8,128)(2,1)} %pad_maximum_fusion.1), channel_id=1, source_target_pairs={{2,0},{4,2},{6,4},{8,6},{10,8},{12,10},{14,12},{16,14},{18,16},{20... | collective-permute-start | bytes 3145736 | tf_op jit(solution)/shard_map/ppermute | solution.py:23
  7.6 3.6 %collective-permute-start.1 = (bf16[1024,512]{1,0:T(8,128)(2,1)}, bf16[1024,512]{1,0:T(8,128)(2,1)}, u32[]{:S(2)}, u32[]{:S(2)}) collective-permute-start(bf16[1024,512]{1,0:T(8,128)(2,1)} %pad_maximum_fusion.1), channel_id=1, source_target_pairs={{0,2},{2,4},{4,6},{6,8},{8,10},{10,12},{12,14},{14,16},{16,18},{18... | collective-permute-start | bytes 3145736 | tf_op jit(solution)/shard_map/ppermute | solution.py:23
  11.2 1.1 pad_maximum_fusion.2
  12.2 1.9 collective-permute-start.4
  14.1 4.5 %collective-permute-start.3 = (bf16[1024,512]{1,0:T(8,128)(2,1)}, bf16[1024,512]{1,0:T(8,128)(2,1)}, u32[]{:S(2)}, u32[]{:S(2)}) collective-permute-start(bf16[1024,512]{1,0:T(8,128)(2,1)} %pad_maximum_fusion.2), channel_id=1, source_target_pairs={{0,2},{2,4},{4,6},{6,8},{8,10},{10,12},{12,14},{14,16},{16,18},{18... | collective-permute-start | bytes 3145736 | tf_op jit(solution)/shard_map/ppermute | solution.py:23
  18.7 0.1 dynamic_slice.7.active
  18.8 0.1 constant_dynamic-slice_fusion
  18.9 0.1 copy.13
  18.9 0.1 reshape.11.places
  19.0 6.0 %collective-permute-done = bf16[1024,512]{1,0:T(8,128)(2,1)S(1)} collective-permute-done((bf16[1024,512]{1,0:T(8,128)(2,1)}, bf16[1024,512]{1,0:T(8,128)(2,1)S(1)}, u32[]{:S(2)}, u32[]{:S(2)}) %collective-permute-start) | collective-permute-done | bytes 1048608 | tf_op jit(solution)/shard_map/ppermute | solution.py:410
  25.1 0.1 broadcast_select_fusion.1
  25.2 1.3 convolution_convert_fusion.g_ref
  26.5 41.4 %shard_map.102 = (bf16[1024,256]{1,0:T(8,128)(2,1)S(1)}, bf16[1024,256]{1,0:T(8,128)(2,1)S(1)}, bf16[1024,512]{1,0:T(8,128)(2,1)S(1)}, f32[1024,512]{1,0:T(8,128)}, bf16[1024,512]{1,0:T(8,128)(2,1)S(1)}) custom-call(s32[96]{0:T(128)S(1)} %reshape.11.places, s32[8]{0:T(128)S(1)} %dynamic_slice.7.active, bf16[1024,512]{1,0:T(8,128)(2,1)S(1)} %copy-done.1, ...), custom_call_target="tpu_custom_call" | custom-call | flops 11274289152 | bytes 8388608 | tf_op jit(solution)/shard_map/pallas_call | solution.py:228
  67.9 21.6 %collective-permute-start.5 = (bf16[1024,512]{1,0:T(8,128)(2,1)S(1)}, bf16[1024,512]{1,0:T(8,128)(2,1)S(1)}, u32[]{:S(2)}, u32[]{:S(2)}) collective-permute-start(bf16[1024,512]{1,0:T(8,128)(2,1)S(1)} %get-tuple-element.17), channel_id=1, source_target_pairs={{2,0},{4,2},{6,4},{8,6},{10,8},{12,10},{14,12},{16,14},{18,16},{20... | collective-permute-start | bytes 3145736 | tf_op jit(solution)/shard_map/ppermute | solution.py:23
  89.6 1.9 collective-permute-start.6
  91.5 41.5 %shard_map.103 = (bf16[1024,256]{1,0:T(8,128)(2,1)S(1)}, bf16[1024,256]{1,0:T(8,128)(2,1)S(1)}, bf16[1024,512]{1,0:T(8,128)(2,1)S(1)}, f32[1024,512]{1,0:T(8,128)}, bf16[1024,512]{1,0:T(8,128)(2,1)S(1)}) custom-call(s32[96]{0:T(128)S(1)} %reshape.11.places, s32[8]{0:T(128)S(1)} %dynamic_slice.7.active, bf16[1024,512]{1,0:T(8,128)(2,1)S(1)} %copy-done.1, ...), custom_call_target="tpu_custom_call" | custom-call | flops 11274289152 | bytes 8388608 | tf_op jit(solution)/shard_map/pallas_call | solution.py:228
  133.0 3.4 %collective-permute-start.7 = (bf16[1024,512]{1,0:T(8,128)(2,1)S(1)}, bf16[1024,512]{1,0:T(8,128)(2,1)S(1)}, u32[]{:S(2)}, u32[]{:S(2)}) collective-permute-start(bf16[1024,512]{1,0:T(8,128)(2,1)S(1)} %get-tuple-element.20), channel_id=1, source_target_pairs={{2,0},{4,2},{6,4},{8,6},{10,8},{12,10},{14,12},{16,14},{18,16},{20... | collective-permute-start | bytes 3145736 | tf_op jit(solution)/shard_map/ppermute | solution.py:23
  136.4 3.1 %collective-permute-start.8 = (bf16[1024,512]{1,0:T(8,128)(2,1)S(1)}, bf16[1024,512]{1,0:T(8,128)(2,1)S(1)}, u32[]{:S(2)}, u32[]{:S(2)}) collective-permute-start(bf16[1024,512]{1,0:T(8,128)(2,1)S(1)} %get-tuple-element.21), channel_id=1, source_target_pairs={{0,2},{2,4},{4,6},{6,8},{8,10},{10,12},{12,14},{14,16},{16,18},{18... | collective-permute-start | bytes 3145736 | tf_op jit(solution)/shard_map/ppermute | solution.py:23
  139.5 0.7 fusion.1.refs_0_
  140.2 0.7 fusion.refs_1_
  141.0 43.3 %shard_map.104 = bf16[512,1024]{1,0:T(8,128)(2,1)S(1)} custom-call(f32[256,1024]{1,0:T(8,128)S(1)} %fusion.1.refs_0_, f32[256,1024]{1,0:T(8,128)S(1)} %fusion.refs_1_), custom_call_target="tpu_custom_call" | custom-call | flops 2097152 | bytes 20971520 | tf_op jit(solution)/shard_map/pallas_call | solution.py:370
  184.2 1.1 pad_maximum_fusion.3
  185.3 1.6 convert_multiply_fusion
  186.9 0.7 copy-done.2
  187.6 0.4 add_convert_fusion.1
  188.2 1.5 copy-done.3
  189.7 0.4 add_convert_fusion
  190.2 1.1 pad_maximum_fusion.5
  191.3 1.1 pad_maximum_fusion.4
  (23 shorter events, 0.2 us)
Async XLA Ops:
  0.6 24.6 %copy-start = (bf16[512,1024]{1,0:T(8,128)(2,1)S(1)}, bf16[512,1024]{1,0:T(8,128)(2,1)}, u32[]{:S(2)}) copy-start(bf16[512,1024]{1,0:T(8,128)(2,1)} %param.11) | copy-start | bytes 3145732
  0.6 24.4 %collective-permute-start = (bf16[1024,512]{1,0:T(8,128)(2,1)}, bf16[1024,512]{1,0:T(8,128)(2,1)S(1)}, u32[]{:S(2)}, u32[]{:S(2)}) collective-permute-start(bf16[1024,512]{1,0:T(8,128)(2,1)} %param.10), channel_id=1, source_target_pairs={{0,1},{1,0},{2,3},{3,2},{4,5},{5,4},{6,7},{7,6},{8,9},{9,8},{10,11... | collective-permute-start | bytes 3145736 | tf_op jit(solution)/shard_map/ppermute | solution.py:410
  3.6 15.1 %copy-start.6 = (s32[128]{0:T(128)S(1)}, s32[128]{0:T(128)}, u32[]{:S(2)}) copy-start(s32[128]{0:T(128)} %param.13) | copy-start | bytes 1540
  3.6 15.2 %copy-start.5 = (s32[128,12]{0,1:T(8,128)S(1)}, s32[128,12]{0,1:T(8,128)}, u32[]{:S(2)}) copy-start(s32[128,12]{0,1:T(8,128)} %param.12) | copy-start | bytes 18436
  3.6 21.4 %copy-start.4 = (bf16[1024,512]{1,0:T(8,128)(2,1)S(1)}, bf16[1024,512]{1,0:T(8,128)(2,1)}, u32[]{:S(2)}) copy-start(bf16[1024,512]{1,0:T(8,128)(2,1)} %param.10) | copy-start | bytes 3145732
  4.7 21.8 %collective-permute-start.2 = (bf16[1024,512]{1,0:T(8,128)(2,1)}, bf16[1024,512]{1,0:T(8,128)(2,1)}, u32[]{:S(2)}, u32[]{:S(2)}) collective-permute-start(bf16[1024,512]{1,0:T(8,128)(2,1)} %pad_maximum_fusion.1), channel_id=1, source_target_pairs={{2,0},{4,2},{6,4},{8,6},{10,8},{12,10},{14,12},{16,14},{18,16},{20... | collective-permute-start | bytes 3145736 | tf_op jit(solution)/shard_map/ppermute | solution.py:23
  7.6 19.0 %collective-permute-start.1 = (bf16[1024,512]{1,0:T(8,128)(2,1)}, bf16[1024,512]{1,0:T(8,128)(2,1)}, u32[]{:S(2)}, u32[]{:S(2)}) collective-permute-start(bf16[1024,512]{1,0:T(8,128)(2,1)} %pad_maximum_fusion.1), channel_id=1, source_target_pairs={{0,2},{2,4},{4,6},{6,8},{8,10},{10,12},{12,14},{14,16},{16,18},{18... | collective-permute-start | bytes 3145736 | tf_op jit(solution)/shard_map/ppermute | solution.py:23
  12.2 79.3 %collective-permute-start.4 = (bf16[1024,512]{1,0:T(8,128)(2,1)}, bf16[1024,512]{1,0:T(8,128)(2,1)}, u32[]{:S(2)}, u32[]{:S(2)}) collective-permute-start(bf16[1024,512]{1,0:T(8,128)(2,1)} %pad_maximum_fusion.2), channel_id=1, source_target_pairs={{2,0},{4,2},{6,4},{8,6},{10,8},{12,10},{14,12},{16,14},{18,16},{20... | collective-permute-start | bytes 3145736 | tf_op jit(solution)/shard_map/ppermute | solution.py:23
  14.1 77.4 %collective-permute-start.3 = (bf16[1024,512]{1,0:T(8,128)(2,1)}, bf16[1024,512]{1,0:T(8,128)(2,1)}, u32[]{:S(2)}, u32[]{:S(2)}) collective-permute-start(bf16[1024,512]{1,0:T(8,128)(2,1)} %pad_maximum_fusion.2), channel_id=1, source_target_pairs={{0,2},{2,4},{4,6},{6,8},{8,10},{10,12},{12,14},{14,16},{16,18},{18... | collective-permute-start | bytes 3145736 | tf_op jit(solution)/shard_map/ppermute | solution.py:23
  25.2 1.3 copy-start.1
  67.9 119.0 %collective-permute-start.5 = (bf16[1024,512]{1,0:T(8,128)(2,1)S(1)}, bf16[1024,512]{1,0:T(8,128)(2,1)S(1)}, u32[]{:S(2)}, u32[]{:S(2)}) collective-permute-start(bf16[1024,512]{1,0:T(8,128)(2,1)S(1)} %get-tuple-element.17), channel_id=1, source_target_pairs={{2,0},{4,2},{6,4},{8,6},{10,8},{12,10},{14,12},{16,14},{18,16},{20... | collective-permute-start | bytes 3145736 | tf_op jit(solution)/shard_map/ppermute | solution.py:23
  89.6 97.3 %collective-permute-start.6 = (bf16[1024,512]{1,0:T(8,128)(2,1)S(1)}, bf16[1024,512]{1,0:T(8,128)(2,1)S(1)}, u32[]{:S(2)}, u32[]{:S(2)}) collective-permute-start(bf16[1024,512]{1,0:T(8,128)(2,1)S(1)} %get-tuple-element.18), channel_id=1, source_target_pairs={{0,2},{2,4},{4,6},{6,8},{8,10},{10,12},{12,14},{14,16},{16,18},{18... | collective-permute-start | bytes 3145736 | tf_op jit(solution)/shard_map/ppermute | solution.py:23
  133.0 55.1 %collective-permute-start.7 = (bf16[1024,512]{1,0:T(8,128)(2,1)S(1)}, bf16[1024,512]{1,0:T(8,128)(2,1)S(1)}, u32[]{:S(2)}, u32[]{:S(2)}) collective-permute-start(bf16[1024,512]{1,0:T(8,128)(2,1)S(1)} %get-tuple-element.20), channel_id=1, source_target_pairs={{2,0},{4,2},{6,4},{8,6},{10,8},{12,10},{14,12},{16,14},{18,16},{20... | collective-permute-start | bytes 3145736 | tf_op jit(solution)/shard_map/ppermute | solution.py:23
  136.4 51.8 %collective-permute-start.8 = (bf16[1024,512]{1,0:T(8,128)(2,1)S(1)}, bf16[1024,512]{1,0:T(8,128)(2,1)S(1)}, u32[]{:S(2)}, u32[]{:S(2)}) collective-permute-start(bf16[1024,512]{1,0:T(8,128)(2,1)S(1)} %get-tuple-element.21), channel_id=1, source_target_pairs={{0,2},{2,4},{4,6},{6,8},{8,10},{10,12},{12,14},{14,16},{16,18},{18... | collective-permute-start | bytes 3145736 | tf_op jit(solution)/shard_map/ppermute | solution.py:23
  185.3 2.3 %copy-start.2 = (f32[1024,512]{1,0:T(8,128)S(1)}, f32[1024,512]{1,0:T(8,128)}, u32[]{:S(2)}) copy-start(f32[1024,512]{1,0:T(8,128)} %get-tuple-element.16) | copy-start | bytes 6291460
  188.1 1.6 copy-start.3

commit v3 on v2

--- a/solution.py
+++ b/solution.py
@@ -10,7 +10,7 @@
 HD = 64
 BS = 128
 LANES = 2 * HD
-STEP = 2
+STEPS = (4, 2)
 FACTOR = HD ** (-0.5)
 
 def mm(a, b):
@@ -37,33 +37,33 @@
 def attention_kernel(
     places,
     active,
-    q_ref,
-    g_ref,
-    k_mid,
-    v_mid,
-    left_ref,
-    right_ref,
-    att_ref,
-    dq_ref,
-    out_left,
-    out_mid,
-    out_right,
-    kw,
-    vw,
-    kt,
-    vt,
-    fixed,
-    fixed_t,
-    sc,
-    peak,
-    mass,
-    dk,
-    dv,
-    *,
+    *refs,
     blocks,
     slots,
     pairs,
 ):
+    q_refs, g_refs, k_mids, v_mids = [refs[i * pairs : (i + 1) * pairs] for i in range(4)]
+    (
+        left_ref,
+        right_ref,
+        att_ref,
+        dq_ref,
+        out_left,
+        out_mid,
+        out_right,
+        kw,
+        vw,
+        kt,
+        vt,
+        fixed,
+        fixed_t,
+        sc,
+        peak,
+        mass,
+        acc,
+        dk,
+        dv,
+    ) = refs[4 * pairs :]
     block = pl.program_id(0)
     width = pairs * LANES
 
@@ -80,7 +80,7 @@
                 for part, (kr, kc, vr, vc) in enumerate(
                     (
                         (left_ref, cols, left_ref, vcols),
-                        (k_mid, cols, v_mid, cols),
+                        (k_mids[p], slice(None), v_mids[p], slice(None)),
                         (right_ref, cols, right_ref, vcols),
                     )
                 ):
@@ -96,15 +96,28 @@
         lax.fori_loop(0, blocks, place_block, 0)
 
     count = active[block]
-    trips = (count + STEP - 1) // STEP
+    large, small = STEPS
+    full = (count + 1) // large
+    rest = (jnp.maximum(count - full * large, 0) + small - 1) // small
     base = block * slots
-    chunk = STEP * BS
+
+    def sweep(visit):
+        def large_trip(t, carry):
+            visit(t * large, large)
+            return carry
+
+        def small_trip(t, carry):
+            visit(full * large + t * small, small)
+            return carry
+
+        lax.fori_loop(0, full, large_trip, 0)
+        lax.fori_loop(0, rest, small_trip, 0)
 
     q_cols, g_cols, gt = [], [], []
     for p in range(pairs):
         cols = slice(p * LANES, (p + 1) * LANES)
-        q = q_ref[:, cols].astype(jnp.float32)
-        g = g_ref[:, cols].astype(jnp.float32)
+        q = q_refs[p][...].astype(jnp.float32)
+        g = g_refs[p][...].astype(jnp.float32)
         gt.append(g.T)
         fixed[p, 0] = stacked(q, 1)
         fixed[p, 1] = stacked(g, 1)
@@ -114,51 +127,48 @@
         fixed_t[p, 0] = q_cols[p]
         fixed_t[p, 1] = g_cols[p]
 
-    def slot_places(t):
-        return [places[base + t * STEP + u] for u in range(STEP)]
+    def slot_places(start, step):
+        return [places[base + start + u] for u in range(step)]
 
     for p in range(pairs):
         peak[p] = jnp.full(peak.shape[1:], -1e30, jnp.float32)
         mass[p] = jnp.zeros(mass.shape[1:], jnp.float32)
 
-    def score_step(t, carry):
-        at = slot_places(t)
+    def score_step(start, step):
+        at = slot_places(start, step)
         for p in range(pairs):
             both = mm(jnp.concatenate([kw[p, a] for a in at], axis=0), fixed_t[p, 0])
-            for u in range(STEP):
-                slot = t * STEP + u
-                rows = pl.ds(pl.multiple_of(t * chunk + u * BS, BS), BS)
+            for u in range(step):
+                slot = start + u
+                rows = pl.ds(pl.multiple_of(slot * BS, BS), BS)
                 s = both[u * BS : (u + 1) * BS]
                 m = jnp.max(s, axis=0, keepdims=True)
                 e = jnp.exp(s - m)
                 sc[p, rows, :] = e
                 peak[p, pl.ds(slot, 1), :] = jnp.where(slot < count, m, -1e30)
                 mass[p, pl.ds(slot, 1), :] = jnp.sum(e, axis=0, keepdims=True)
-        return carry
-
-    lax.fori_loop(0, trips, score_step, 0)
+
+    sweep(score_step)
     for p in range(pairs):
         ratio = jnp.exp(peak[p] - jnp.max(peak[p], axis=0, keepdims=True))
         total = jnp.sum(mass[p] * ratio, axis=0, keepdims=True)
         peak[p] = ratio * (1.0 / total)
 
-    def weights(p, t, u):
-        rows = pl.ds(pl.multiple_of(t * chunk + u * BS, BS), BS)
-        return sc[p, rows, :] * peak[p, pl.ds(t * STEP + u, 1), :]
-
-    def sum_step(t, acc):
-        at = slot_places(t)
-        acc = list(acc)
+    def weights(p, slot):
+        rows = pl.ds(pl.multiple_of(slot * BS, BS), BS)
+        return sc[p, rows, :] * peak[p, pl.ds(slot, 1), :]
+
+    def sum_step(start, step):
+        at = slot_places(start, step)
         for p in range(pairs):
             w = jnp.concatenate(
-                [weights(p, t, u).astype(jnp.bfloat16) for u in range(STEP)], axis=0
+                [weights(p, start + u).astype(jnp.bfloat16) for u in range(step)], axis=0
             )
             v_t = jnp.concatenate([vt[p, a] for a in at], axis=1)
-            acc[p] = acc[p] + mm(v_t, w)
-        return tuple(acc)
-
-    blank = jnp.zeros((LANES, 2 * BS), jnp.float32)
-    acc = lax.fori_loop(0, trips, sum_step, (blank,) * pairs)
+            acc[p] += mm(v_t, w)
+
+    acc[...] = jnp.zeros_like(acc)
+    sweep(sum_step)
     dots = []
     for p in range(pairs):
         cols = slice(p * LANES, (p + 1) * LANES)
@@ -175,25 +185,24 @@
             )
         )
 
-    def grad_step(t, acc):
-        at = slot_places(t)
-        acc = list(acc)
+    def grad_step(start, step):
+        at = slot_places(start, step)
         for p in range(pairs):
             dp = mm(jnp.concatenate([vw[p, a] for a in at], axis=0), fixed_t[p, 1])
-            w = [weights(p, t, u) for u in range(STEP)]
-            ds = [w[u] * (dp[u * BS : (u + 1) * BS] - dots[p]) for u in range(STEP)]
+            w = [weights(p, start + u) for u in range(step)]
+            ds = [w[u] * (dp[u * BS : (u + 1) * BS] - dots[p]) for u in range(step)]
             w = jnp.concatenate(w, axis=0).astype(jnp.bfloat16)
             ds = jnp.concatenate(ds, axis=0).astype(jnp.bfloat16)
             grad_v = mm(w, fixed[p, 1])
             grad_k = mm(ds, fixed[p, 0])
             k_t = jnp.concatenate([kt[p, a] for a in at], axis=1)
-            acc[p] = acc[p] + mm(k_t, ds)
-            for u in range(STEP):
+            acc[p] += mm(k_t, ds)
+            for u in range(step):
                 dv[p, at[u]] += grad_v[u * BS : (u + 1) * BS]
                 dk[p, at[u]] += grad_k[u * BS : (u + 1) * BS]
-        return tuple(acc)
-
-    acc = lax.fori_loop(0, trips, grad_step, (blank,) * pairs)
+
+    acc[...] = jnp.zeros_like(acc)
+    sweep(grad_step)
     for p in range(pairs):
         cols = slice(p * LANES, (p + 1) * LANES)
         dq_ref[:, cols] = (own_parts(acc[p]).T * FACTOR).astype(jnp.bfloat16)
@@ -214,23 +223,23 @@
         lax.fori_loop(0, blocks, put_block, 0)
 
 
-def group_attention(places, active, queries, grads, keys, values, left, right, group, pairs):
+def group_attention(places, active, queries, grads, keys, values, left, right, start, pairs):
     rows = queries.shape[0]
     blocks = rows // BS
     slots = places.shape[0] // blocks
     width = pairs * LANES
-    tile = pl.BlockSpec((BS, width), lambda i, *_: (i, group))
-    whole = pl.BlockSpec((rows, width), lambda i, *_: (0, group))
+    tiles = [pl.BlockSpec((BS, LANES), lambda i, *_, at=start + p: (i, at)) for p in range(pairs)]
+    wholes = [pl.BlockSpec((rows, LANES), lambda i, *_, at=start + p: (0, at)) for p in range(pairs)]
     out_tile = pl.BlockSpec((BS, width), lambda i, *_: (i, 0))
     packed = pl.BlockSpec((rows, 2 * width), lambda i, *_: (0, 0))
     window = (pairs, 3 * blocks, BS, LANES)
-    padded = (slots + STEP - 1) // STEP * STEP
+    padded = slots
     return pl.pallas_call(
         functools.partial(attention_kernel, blocks=blocks, slots=slots, pairs=pairs),
         grid_spec=pltpu.PrefetchScalarGridSpec(
             num_scalar_prefetch=2,
             grid=(blocks,),
-            in_specs=[tile, tile, whole, whole, packed, packed],
+            in_specs=[*tiles, *tiles, *wholes, *wholes, packed, packed],
             out_specs=[out_tile, out_tile, packed, packed, packed],
             scratch_shapes=[
                 pltpu.VMEM(window, jnp.bfloat16),
@@ -242,6 +251,7 @@
                 pltpu.VMEM((pairs, padded * BS, 2 * BS), jnp.float32),
                 pltpu.VMEM((pairs, (padded + 7) // 8 * 8, 2 * BS), jnp.float32),
                 pltpu.VMEM((pairs, (padded + 7) // 8 * 8, 2 * BS), jnp.float32),
+                pltpu.VMEM((pairs, LANES, 2 * BS), jnp.float32),
                 pltpu.VMEM(window, jnp.float32),
                 pltpu.VMEM(window, jnp.float32),
             ],
@@ -261,7 +271,16 @@
             bytes_accessed=rows * width * 32,
             transcendentals=2 * blocks * slots * pairs * BS * BS,
         ),
-    )(places, active, queries, grads, keys, values, left, right)
+    )(
+        places,
+        active,
+        *[queries] * pairs,
+        *[grads] * pairs,
+        *[keys] * pairs,
+        *[values] * pairs,
+        left,
+        right,
+    )
 
 
 def sum_kernel(*refs, sizes, count):
@@ -394,15 +413,14 @@
     blocks = row_count // BS
     slots = neighbours.shape[1]
     pair_total = col_count // LANES
-    pairs = 2 if pair_total % 2 == 0 else 1
-    groups = pair_total // pairs
-    width = pairs * LANES
+    groups = [1, 2, 1] if pair_total == 4 else [1] * pair_total
+    starts = [sum(groups[:g]) for g in range(len(groups))]
     ctx_index = lax.axis_index("ctx")
     head_index = lax.axis_index("head")
 
     halos = []
-    for g in range(groups):
-        cols = slice(g * width, (g + 1) * width)
+    for start, pairs in zip(starts, groups):
+        cols = slice(start * LANES, (start + pairs) * LANES)
         packed = jnp.concatenate([key_rows[:, cols], value_rows[:, cols]], axis=1)
         halos.append((shifted(packed, "ctx", 1), shifted(packed, "ctx", -1)))
 
@@ -421,14 +439,15 @@
     listed = lax.dynamic_slice_in_dim(neighbours, first_block, blocks, axis=0)
     active = lax.dynamic_slice_in_dim(counts, first_block, blocks, axis=0)
     places = jnp.clip(listed - (first_block - blocks), 0, 3 * blocks - 1)
-    if slots % STEP:
-        places = jnp.concatenate([places, places[:, :1]], axis=1)
+    if slots % STEPS[0]:
+        extra = STEPS[0] - slots % STEPS[0]
+        places = jnp.concatenate([places] + [places[:, :1]] * extra, axis=1)
     places = places.reshape(-1)
     scale = (row_count * lax.axis_size("ctx")) ** (-0.5)
 
     query_parts, key_parts, value_parts, weight_parts = [], [], [], []
-    for g in range(groups):
-        left, right = halos[g]
+    for (left, right), start, pairs in zip(halos, starts, groups):
+        width = pairs * LANES
         attended, dq, to_left, middle, to_right = group_attention(
             places,
             active,
@@ -438,7 +457,7 @@
             value_rows,
             left,
             right,
-            g,
+            start,
             pairs,
         )
         product = jnp.einsum("rj,ro->jo", attended, cotangent, preferred_element_type=jnp.float32)

time: 191 us -> 199 us (1.042)
  Pallas kernels: 126 us -> 102 us
  starting transfers between devices: 44.2 us -> 63.8 us
  waiting for transfers between devices: 6.05 us -> 13 us
  other arithmetic: 7.91 us -> 10.1 us
    pallas_call x2 -> x3, Pallas kernels: 82.9 us -> 48.3 us  [group_attention(): pl.pallas_call(functools.partial(attention_kernel, blocks=blocks, slots=s...]
    ppermute x8 -> x12, starting transfers between devices: 42.9 us -> 62.5 us  [shifted(): return lax.ppermute(x, axis, pairs)]
    ppermute x8 -> x12, waiting for transfers between devices: 0.02 us -> 11.3 us  [shifted(): return lax.ppermute(x, axis, pairs)]
    pallas_call x1, Pallas kernels: 43.3 us -> 54 us  [summed_over_ctx(): pl.pallas_call(functools.partial(sum_kernel, sizes=sizes, count=len(parts...]
    ppermute x1, waiting for transfers between devices: 6.03 us -> 1.72 us  [body(): other = lax.ppermute(out_grad, 'head', [(0, 1), (1, 0)])]
    slice x1 -> x3, local copies, waits for them, and re-layouts: 1.65 us -> 5.02 us  [body(): packed = jnp.concatenate([key_rows[:, cols], value_rows[:, cols]], axis=1)]
    unnamed x15, local copies, waits for them, and re-layouts: 2.34 us -> 0.12 us
  transfers between devices with their start and end apart: 9 -> 13, of which waited for: 1 -> 2; matrix products, arithmetic and copies ran while one was open for 5% -> 8% of each run, Pallas kernels for 66% -> 51%
where the time goes in v3:
time: 199 us
  Pallas kernels  102 us (51%)
  starting transfers between devices  63.8 us (32%)
  waiting for transfers between devices  13 us (7%)
  other arithmetic  10.1 us (5%)
  local copies, waits for them, and re-layouts  5.52 us (3%)
  matrix products  2.95 us (1%)
    ppermute x12, starting transfers between devices, shifted(): return lax.ppermute(x, axis, pairs)  62.5 us
    pallas_call x1, Pallas kernels, summed_over_ctx(): pl.pallas_call(functools.partial(sum_kernel, sizes=sizes, count=len(parts...  54 us
    pallas_call x3, Pallas kernels, group_attention(): pl.pallas_call(functools.partial(attention_kernel, blocks=blocks, slots=s...  48.3 us
    ppermute x12, waiting for transfers between devices, shifted(): return lax.ppermute(x, axis, pairs)  11.3 us
    slice x3, local copies, waits for them, and re-layouts, body(): packed = jnp.concatenate([key_rows[:, cols], value_rows[:, cols]], axis=1)  5.02 us
  transfers between devices with their start and end apart: 13, of which 2 were waited for; matrix products, arithmetic and copies ran while one was open for 8% of the time, Pallas kernels for 51%

profile of v3, /device:TPU:11, one launch (start us, length us, event | category | flops | bytes accessed | tf_op | source)
XLA Modules:
  0.0 198.7 jit_solution(17488031052046281120)
XLA Ops:
  0.6 1.3 collective-permute-start
  2.0 1.3 fusion.4
  3.3 0.9 pad_maximum_fusion.6
  4.1 2.9 %collective-permute-start.6 = (bf16[1024,256]{1,0:T(8,128)(2,1)}, bf16[1024,256]{1,0:T(8,128)(2,1)S(1)}, u32[]{:S(2)}, u32[]{:S(2)}) collective-permute-start(bf16[1024,256]{1,0:T(8,128)(2,1)} %pad_maximum_fusion.6), channel_id=1, source_target_pairs={{2,0},{4,2},{6,4},{8,6},{10,8},{12,10},{14,12},{16,14},{18,16},{20... | collective-permute-start | bytes 1572872 | tf_op jit(solution)/shard_map/ppermute | solution.py:23
  7.0 3.6 %collective-permute-start.5 = (bf16[1024,256]{1,0:T(8,128)(2,1)}, bf16[1024,256]{1,0:T(8,128)(2,1)S(1)}, u32[]{:S(2)}, u32[]{:S(2)}) collective-permute-start(bf16[1024,256]{1,0:T(8,128)(2,1)} %pad_maximum_fusion.6), channel_id=1, source_target_pairs={{0,2},{2,4},{4,6},{6,8},{8,10},{10,12},{12,14},{14,16},{16,18},{18... | collective-permute-start | bytes 1572872 | tf_op jit(solution)/shard_map/ppermute | solution.py:23
  10.6 0.9 pad_maximum_fusion.5
  11.4 1.9 collective-permute-start.2
  13.3 4.5 %collective-permute-start.1 = (bf16[1024,256]{1,0:T(8,128)(2,1)}, bf16[1024,256]{1,0:T(8,128)(2,1)S(1)}, u32[]{:S(2)}, u32[]{:S(2)}) collective-permute-start(bf16[1024,256]{1,0:T(8,128)(2,1)} %pad_maximum_fusion.5), channel_id=1, source_target_pairs={{0,2},{2,4},{4,6},{6,8},{8,10},{10,12},{12,14},{14,16},{16,18},{18... | collective-permute-start | bytes 1572872 | tf_op jit(solution)/shard_map/ppermute | solution.py:23
  17.9 1.9 slice.38
  19.8 1.9 slice.39
  22.0 1.4 pad_maximum_fusion.1
  23.3 1.7 collective-permute-done
  25.1 3.4 %collective-permute-start.4 = (bf16[1024,512]{1,0:T(8,128)(2,1)S(1)}, bf16[1024,512]{1,0:T(8,128)(2,1)S(1)}, u32[]{:S(2)}, u32[]{:S(2)}) collective-permute-start(bf16[1024,512]{1,0:T(8,128)(2,1)S(1)} %pad_maximum_fusion.1), channel_id=1, source_target_pairs={{2,0},{4,2},{6,4},{8,6},{10,8},{12,10},{14,12},{16,14},{18,16},{20... | collective-permute-start | bytes 3145736 | tf_op jit(solution)/shard_map/ppermute | solution.py:23
  28.5 1.4 broadcast_select_fusion.1
  29.9 1.3 convolution_convert_fusion.refs_1_.refs_2_.refs_3_
  31.2 3.1 %collective-permute-start.3 = (bf16[1024,512]{1,0:T(8,128)(2,1)S(1)}, bf16[1024,512]{1,0:T(8,128)(2,1)}, u32[]{:S(2)}, u32[]{:S(2)}) collective-permute-start(bf16[1024,512]{1,0:T(8,128)(2,1)S(1)} %pad_maximum_fusion.1), channel_id=1, source_target_pairs={{0,2},{2,4},{4,6},{6,8},{8,10},{10,12},{12,14},{14,16},{16,18},{18... | collective-permute-start | bytes 3145736 | tf_op jit(solution)/shard_map/ppermute | solution.py:23
  34.3 13.6 %shard_map.104 = (bf16[1024,128]{1,0:T(8,128)(2,1)S(1)}, bf16[1024,128]{1,0:T(8,128)(2,1)S(1)}, bf16[1024,256]{1,0:T(8,128)(2,1)S(1)}, f32[1024,256]{1,0:T(8,128)S(1)}, bf16[1024,256]{1,0:T(8,128)(2,1)S(1)}) custom-call(s32[96]{0:T(128)S(1)} %reshape.11.places, s32[8]{0:T(128)S(1)} %dynamic_slice.7.active, bf16[1024,512]{1,0:T(8,128)(2,1)S(1)} %copy-done.1, ...), custom_call_target="tpu_custom_call" | custom-call | flops 5637144576 | bytes 4194304 | tf_op jit(solution)/shard_map/pallas_call | solution.py:237
  47.9 9.0 %collective-permute-start.11 = (bf16[1024,256]{1,0:T(8,128)(2,1)S(1)}, bf16[1024,256]{1,0:T(8,128)(2,1)S(1)}, u32[]{:S(2)}, u32[]{:S(2)}) collective-permute-start(bf16[1024,256]{1,0:T(8,128)(2,1)S(1)} %get-tuple-element.29), channel_id=1, source_target_pairs={{2,0},{4,2},{6,4},{8,6},{10,8},{12,10},{14,12},{16,14},{18,16},{20... | collective-permute-start | bytes 1572872 | tf_op jit(solution)/shard_map/ppermute | solution.py:23
  56.9 1.9 collective-permute-start.12
  58.8 13.6 %shard_map.102 = (bf16[1024,128]{1,0:T(8,128)(2,1)S(1)}, bf16[1024,128]{1,0:T(8,128)(2,1)S(1)}, bf16[1024,256]{1,0:T(8,128)(2,1)S(1)}, f32[1024,256]{1,0:T(8,128)S(1)}, bf16[1024,256]{1,0:T(8,128)(2,1)S(1)}) custom-call(s32[96]{0:T(128)S(1)} %reshape.11.places, s32[8]{0:T(128)S(1)} %dynamic_slice.7.active, bf16[1024,512]{1,0:T(8,128)(2,1)S(1)} %copy-done.1, ...), custom_call_target="tpu_custom_call" | custom-call | flops 5637144576 | bytes 4194304 | tf_op jit(solution)/shard_map/pallas_call | solution.py:237
  72.5 10.2 %collective-permute-start.7 = (bf16[1024,256]{1,0:T(8,128)(2,1)S(1)}, bf16[1024,256]{1,0:T(8,128)(2,1)S(1)}, u32[]{:S(2)}, u32[]{:S(2)}) collective-permute-start(bf16[1024,256]{1,0:T(8,128)(2,1)S(1)} %get-tuple-element.23), channel_id=1, source_target_pairs={{2,0},{4,2},{6,4},{8,6},{10,8},{12,10},{14,12},{16,14},{18,16},{20... | collective-permute-start | bytes 1572872 | tf_op jit(solution)/shard_map/ppermute | solution.py:23
  83.2 1.9 collective-permute-start.8
  85.1 21.1 %shard_map.103 = (bf16[1024,256]{1,0:T(8,128)(2,1)S(1)}, bf16[1024,256]{1,0:T(8,128)(2,1)S(1)}, bf16[1024,512]{1,0:T(8,128)(2,1)S(1)}, f32[1024,512]{1,0:T(8,128)}, bf16[1024,512]{1,0:T(8,128)(2,1)S(1)}) custom-call(s32[96]{0:T(128)S(1)} %reshape.11.places, s32[8]{0:T(128)S(1)} %dynamic_slice.7.active, bf16[1024,512]{1,0:T(8,128)(2,1)S(1)} %copy-done.1, ...), custom_call_target="tpu_custom_call" | custom-call | flops 11274289152 | bytes 8388608 | tf_op jit(solution)/shard_map/pallas_call | solution.py:237
  106.2 0.7 fusion.1.refs_1_
  107.4 13.7 %collective-permute-start.9 = (bf16[1024,512]{1,0:T(8,128)(2,1)S(1)}, bf16[1024,512]{1,0:T(8,128)(2,1)S(1)}, u32[]{:S(2)}, u32[]{:S(2)}) collective-permute-start(bf16[1024,512]{1,0:T(8,128)(2,1)S(1)} %get-tuple-element.26), channel_id=1, source_target_pairs={{2,0},{4,2},{6,4},{8,6},{10,8},{12,10},{14,12},{16,14},{18,16},{20... | collective-permute-start | bytes 3145736 | tf_op jit(solution)/shard_map/ppermute | solution.py:23
  121.2 54.0 %shard_map.105 = bf16[512,1024]{1,0:T(8,128)(2,1)S(1)} custom-call(f32[128,1024]{1,0:T(8,128)S(1)} %fusion.2.refs_0_, f32[256,1024]{1,0:T(8,128)S(1)} %fusion.1.refs_1_, f32[128,1024]{1,0:T(8,128)S(1)} %fusion.refs_2_), custom_call_target="tpu_custom_call" | custom-call | flops 2097152 | bytes 20971520 | tf_op jit(solution)/shard_map/pallas_call | solution.py:389
  175.2 1.1 pad_maximum_fusion.2
  176.3 1.6 convert_multiply_fusion
  177.9 6.3 %collective-permute-start.10 = (bf16[1024,512]{1,0:T(8,128)(2,1)S(1)}, bf16[1024,512]{1,0:T(8,128)(2,1)S(1)}, u32[]{:S(2)}, u32[]{:S(2)}) collective-permute-start(bf16[1024,512]{1,0:T(8,128)(2,1)S(1)} %get-tuple-element.27), channel_id=1, source_target_pairs={{0,2},{2,4},{4,6},{6,8},{8,10},{10,12},{12,14},{14,16},{16,18},{18... | collective-permute-start | bytes 3145736 | tf_op jit(solution)/shard_map/ppermute | solution.py:23
  184.7 11.2 %collective-permute-done.10 = bf16[1024,512]{1,0:T(8,128)(2,1)S(1)} collective-permute-done((bf16[1024,512]{1,0:T(8,128)(2,1)S(1)}, bf16[1024,512]{1,0:T(8,128)(2,1)S(1)}, u32[]{:S(2)}, u32[]{:S(2)}) %collective-permute-start.10) | collective-permute-done | bytes 1048608 | tf_op jit(solution)/shard_map/ppermute | solution.py:23
  196.5 1.1 pad_maximum_fusion.4
  197.6 1.1 pad_maximum_fusion.3
  (38 shorter events, 2.2 us)
Async XLA Ops:
  0.6 29.3 %copy-start = (bf16[512,1024]{1,0:T(8,128)(2,1)S(1)}, bf16[512,1024]{1,0:T(8,128)(2,1)}, u32[]{:S(2)}) copy-start(bf16[512,1024]{1,0:T(8,128)(2,1)} %param.11) | copy-start | bytes 3145732
  0.6 24.4 %collective-permute-start = (bf16[1024,512]{1,0:T(8,128)(2,1)}, bf16[1024,512]{1,0:T(8,128)(2,1)}, u32[]{:S(2)}, u32[]{:S(2)}) collective-permute-start(bf16[1024,512]{1,0:T(8,128)(2,1)} %param.10), channel_id=1, source_target_pairs={{0,1},{1,0},{2,3},{3,2},{4,5},{5,4},{6,7},{7,6},{8,9},{9,8},{10,11... | collective-permute-start | bytes 3145736 | tf_op jit(solution)/shard_map/ppermute | solution.py:428
  3.2 18.4 %copy-start.6 = (s32[128]{0:T(128)S(1)}, s32[128]{0:T(128)}, u32[]{:S(2)}) copy-start(s32[128]{0:T(128)} %param.13) | copy-start | bytes 1540
  3.2 18.5 %copy-start.4 = (s32[128,12]{0,1:T(8,128)S(1)}, s32[128,12]{0,1:T(8,128)}, u32[]{:S(2)}) copy-start(s32[128,12]{0,1:T(8,128)} %param.12) | copy-start | bytes 18436
  4.1 27.1 %collective-permute-start.6 = (bf16[1024,256]{1,0:T(8,128)(2,1)}, bf16[1024,256]{1,0:T(8,128)(2,1)S(1)}, u32[]{:S(2)}, u32[]{:S(2)}) collective-permute-start(bf16[1024,256]{1,0:T(8,128)(2,1)} %pad_maximum_fusion.6), channel_id=1, source_target_pairs={{2,0},{4,2},{6,4},{8,6},{10,8},{12,10},{14,12},{16,14},{18,16},{20... | collective-permute-start | bytes 1572872 | tf_op jit(solution)/shard_map/ppermute | solution.py:23
  7.0 27.3 %collective-permute-start.5 = (bf16[1024,256]{1,0:T(8,128)(2,1)}, bf16[1024,256]{1,0:T(8,128)(2,1)S(1)}, u32[]{:S(2)}, u32[]{:S(2)}) collective-permute-start(bf16[1024,256]{1,0:T(8,128)(2,1)} %pad_maximum_fusion.6), channel_id=1, source_target_pairs={{0,2},{2,4},{4,6},{6,8},{8,10},{10,12},{12,14},{14,16},{16,18},{18... | collective-permute-start | bytes 1572872 | tf_op jit(solution)/shard_map/ppermute | solution.py:23
  11.4 45.5 %collective-permute-start.2 = (bf16[1024,256]{1,0:T(8,128)(2,1)}, bf16[1024,256]{1,0:T(8,128)(2,1)S(1)}, u32[]{:S(2)}, u32[]{:S(2)}) collective-permute-start(bf16[1024,256]{1,0:T(8,128)(2,1)} %pad_maximum_fusion.5), channel_id=1, source_target_pairs={{2,0},{4,2},{6,4},{8,6},{10,8},{12,10},{14,12},{16,14},{18,16},{20... | collective-permute-start | bytes 1572872 | tf_op jit(solution)/shard_map/ppermute | solution.py:23
  13.3 45.5 %collective-permute-start.1 = (bf16[1024,256]{1,0:T(8,128)(2,1)}, bf16[1024,256]{1,0:T(8,128)(2,1)S(1)}, u32[]{:S(2)}, u32[]{:S(2)}) collective-permute-start(bf16[1024,256]{1,0:T(8,128)(2,1)} %pad_maximum_fusion.5), channel_id=1, source_target_pairs={{0,2},{2,4},{4,6},{6,8},{8,10},{10,12},{12,14},{14,16},{16,18},{18... | collective-permute-start | bytes 1572872 | tf_op jit(solution)/shard_map/ppermute | solution.py:23
  22.0 6.5 %copy-start.3 = (bf16[1024,512]{1,0:T(8,128)(2,1)S(1)}, bf16[1024,512]{1,0:T(8,128)(2,1)}, u32[]{:S(2)}) copy-start(bf16[1024,512]{1,0:T(8,128)(2,1)} %param.10) | copy-start | bytes 3145732
  25.1 58.1 %collective-permute-start.4 = (bf16[1024,512]{1,0:T(8,128)(2,1)S(1)}, bf16[1024,512]{1,0:T(8,128)(2,1)S(1)}, u32[]{:S(2)}, u32[]{:S(2)}) collective-permute-start(bf16[1024,512]{1,0:T(8,128)(2,1)S(1)} %pad_maximum_fusion.1), channel_id=1, source_target_pairs={{2,0},{4,2},{6,4},{8,6},{10,8},{12,10},{14,12},{16,14},{18,16},{20... | collective-permute-start | bytes 3145736 | tf_op jit(solution)/shard_map/ppermute | solution.py:23
  29.9 4.4 %copy-start.1 = (bf16[1024,512]{1,0:T(8,128)(2,1)S(1)}, bf16[1024,512]{1,0:T(8,128)(2,1)}, u32[]{:S(2)}) copy-start(bf16[1024,512]{1,0:T(8,128)(2,1)} %refs_0_.5) | copy-start | bytes 3145732
  31.2 53.9 %collective-permute-start.3 = (bf16[1024,512]{1,0:T(8,128)(2,1)S(1)}, bf16[1024,512]{1,0:T(8,128)(2,1)}, u32[]{:S(2)}, u32[]{:S(2)}) collective-permute-start(bf16[1024,512]{1,0:T(8,128)(2,1)S(1)} %pad_maximum_fusion.1), channel_id=1, source_target_pairs={{0,2},{2,4},{4,6},{6,8},{8,10},{10,12},{12,14},{14,16},{16,18},{18... | collective-permute-start | bytes 3145736 | tf_op jit(solution)/shard_map/ppermute | solution.py:23
  47.9 130.0 %collective-permute-start.11 = (bf16[1024,256]{1,0:T(8,128)(2,1)S(1)}, bf16[1024,256]{1,0:T(8,128)(2,1)S(1)}, u32[]{:S(2)}, u32[]{:S(2)}) collective-permute-start(bf16[1024,256]{1,0:T(8,128)(2,1)S(1)} %get-tuple-element.29), channel_id=1, source_target_pairs={{2,0},{4,2},{6,4},{8,6},{10,8},{12,10},{14,12},{16,14},{18,16},{20... | collective-permute-start | bytes 1572872 | tf_op jit(solution)/shard_map/ppermute | solution.py:23
  56.9 127.3 %collective-permute-start.12 = (bf16[1024,256]{1,0:T(8,128)(2,1)S(1)}, bf16[1024,256]{1,0:T(8,128)(2,1)S(1)}, u32[]{:S(2)}, u32[]{:S(2)}) collective-permute-start(bf16[1024,256]{1,0:T(8,128)(2,1)S(1)} %get-tuple-element.30), channel_id=1, source_target_pairs={{0,2},{2,4},{4,6},{6,8},{8,10},{10,12},{12,14},{14,16},{16,18},{18... | collective-permute-start | bytes 1572872 | tf_op jit(solution)/shard_map/ppermute | solution.py:23
  72.5 112.0 %collective-permute-start.7 = (bf16[1024,256]{1,0:T(8,128)(2,1)S(1)}, bf16[1024,256]{1,0:T(8,128)(2,1)S(1)}, u32[]{:S(2)}, u32[]{:S(2)}) collective-permute-start(bf16[1024,256]{1,0:T(8,128)(2,1)S(1)} %get-tuple-element.23), channel_id=1, source_target_pairs={{2,0},{4,2},{6,4},{8,6},{10,8},{12,10},{14,12},{16,14},{18,16},{20... | collective-permute-start | bytes 1572872 | tf_op jit(solution)/shard_map/ppermute | solution.py:23
  83.2 1.9 copy-start.5
  83.2 101.3 %collective-permute-start.8 = (bf16[1024,256]{1,0:T(8,128)(2,1)S(1)}, bf16[1024,256]{1,0:T(8,128)(2,1)S(1)}, u32[]{:S(2)}, u32[]{:S(2)}) collective-permute-start(bf16[1024,256]{1,0:T(8,128)(2,1)S(1)} %get-tuple-element.24), channel_id=1, source_target_pairs={{0,2},{2,4},{4,6},{6,8},{8,10},{10,12},{12,14},{14,16},{16,18},{18... | collective-permute-start | bytes 1572872 | tf_op jit(solution)/shard_map/ppermute | solution.py:23
  107.4 77.3 %collective-permute-start.9 = (bf16[1024,512]{1,0:T(8,128)(2,1)S(1)}, bf16[1024,512]{1,0:T(8,128)(2,1)S(1)}, u32[]{:S(2)}, u32[]{:S(2)}) collective-permute-start(bf16[1024,512]{1,0:T(8,128)(2,1)S(1)} %get-tuple-element.26), channel_id=1, source_target_pairs={{2,0},{4,2},{6,4},{8,6},{10,8},{12,10},{14,12},{16,14},{18,16},{20... | collective-permute-start | bytes 3145736 | tf_op jit(solution)/shard_map/ppermute | solution.py:23
  177.9 18.1 %collective-permute-start.10 = (bf16[1024,512]{1,0:T(8,128)(2,1)S(1)}, bf16[1024,512]{1,0:T(8,128)(2,1)S(1)}, u32[]{:S(2)}, u32[]{:S(2)}) collective-permute-start(bf16[1024,512]{1,0:T(8,128)(2,1)S(1)} %get-tuple-element.27), channel_id=1, source_target_pairs={{0,2},{2,4},{4,6},{6,8},{8,10},{10,12},{12,14},{14,16},{16,18},{18... | collective-permute-start | bytes 3145736 | tf_op jit(solution)/shard_map/ppermute | solution.py:23
  184.4 11.5 %copy-start.2 = (f32[1024,512]{1,0:T(8,128)S(1)}, f32[1024,512]{1,0:T(8,128)}, u32[]{:S(2)}) copy-start(f32[1024,512]{1,0:T(8,128)} %get-tuple-element.25) | copy-start | bytes 6291460

commit v4 on v3

--- a/solution.py
+++ b/solution.py
@@ -413,7 +413,7 @@
     blocks = row_count // BS
     slots = neighbours.shape[1]
     pair_total = col_count // LANES
-    groups = [1, 2, 1] if pair_total == 4 else [1] * pair_total
+    groups = [2] * (pair_total // 2) + [1] * (pair_total % 2)
     starts = [sum(groups[:g]) for g in range(len(groups))]
     ctx_index = lax.axis_index("ctx")
     head_index = lax.axis_index("head")

time: 199 us -> 171 us (0.86); the launches traced: 199 us -> 168 us
  starting transfers between devices: 63.8 us -> 51 us
  waiting for transfers between devices: 13 us -> 6.05 us
  Pallas kernels: 102 us -> 95.2 us
  other arithmetic: 10.1 us -> 7.91 us
    ppermute x12 -> x8, starting transfers between devices: 62.5 us -> 49.7 us  [shifted(): return lax.ppermute(x, axis, pairs)]
    ppermute x12 -> x8, waiting for transfers between devices: 11.3 us -> 0.02 us  [shifted(): return lax.ppermute(x, axis, pairs)]
    pallas_call x1, Pallas kernels: 54 us -> 44.7 us  [summed_over_ctx(): pl.pallas_call(functools.partial(sum_kernel, sizes=sizes, count=len(parts...]
    ppermute x1, waiting for transfers between devices: 1.72 us -> 6.03 us  [body(): other = lax.ppermute(out_grad, 'head', [(0, 1), (1, 0)])]
    slice x3 -> x1, local copies, waits for them, and re-layouts: 5.02 us -> 1.65 us  [body(): packed = jnp.concatenate([key_rows[:, cols], value_rows[:, cols]], axis=1)]
    unnamed x15, local copies, waits for them, and re-layouts: 0.12 us -> 2.34 us
    pallas_call x3 -> x2, Pallas kernels: 48.3 us -> 50.5 us  [group_attention(): pl.pallas_call(functools.partial(attention_kernel, blocks=blocks, slots=s...]
  transfers between devices with their start and end apart: 13 -> 9, of which waited for: 2 -> 1; matrix products, arithmetic and copies ran while one was open for 8% -> 6% of each run, Pallas kernels for 51% -> 57%
where the time goes in v4:
time: 171 us; the launch traced here: 168 us
  Pallas kernels  95.2 us (56%)
  starting transfers between devices  51 us (30%)
  other arithmetic  7.91 us (5%)
  waiting for transfers between devices  6.05 us (4%)
  local copies, waits for them, and re-layouts  4.36 us (3%)
  matrix products  2.73 us (2%)
    pallas_call x2, Pallas kernels, group_attention(): pl.pallas_call(functools.partial(attention_kernel, blocks=blocks, slots=s...  50.5 us
    ppermute x8, starting transfers between devices, shifted(): return lax.ppermute(x, axis, pairs)  49.7 us
    pallas_call x1, Pallas kernels, summed_over_ctx(): pl.pallas_call(functools.partial(sum_kernel, sizes=sizes, count=len(parts...  44.7 us
    ppermute x1, waiting for transfers between devices, body(): other = lax.ppermute(out_grad, 'head', [(0, 1), (1, 0)])  6.03 us
  transfers between devices with their start and end apart: 9, of which 1 were waited for; matrix products, arithmetic and copies ran while one was open for 6% of the time, Pallas kernels for 57%

profile of v4, /device:TPU:11, one launch (start us, length us, event | category | flops | bytes accessed | tf_op | source)
XLA Modules:
  0.0 168.1 jit_solution(11141539308184775972)
XLA Ops:
  0.6 1.3 collective-permute-start
  2.0 1.7 fusion.7
  3.6 1.1 pad_maximum_fusion.1
  4.7 2.9 %collective-permute-start.2 = (bf16[1024,512]{1,0:T(8,128)(2,1)}, bf16[1024,512]{1,0:T(8,128)(2,1)}, u32[]{:S(2)}, u32[]{:S(2)}) collective-permute-start(bf16[1024,512]{1,0:T(8,128)(2,1)} %pad_maximum_fusion.1), channel_id=1, source_target_pairs={{2,0},{4,2},{6,4},{8,6},{10,8},{12,10},{14,12},{16,14},{18,16},{20... | collective-permute-start | bytes 3145736 | tf_op jit(solution)/shard_map/ppermute | solution.py:23
  7.6 3.6 %collective-permute-start.1 = (bf16[1024,512]{1,0:T(8,128)(2,1)}, bf16[1024,512]{1,0:T(8,128)(2,1)}, u32[]{:S(2)}, u32[]{:S(2)}) collective-permute-start(bf16[1024,512]{1,0:T(8,128)(2,1)} %pad_maximum_fusion.1), channel_id=1, source_target_pairs={{0,2},{2,4},{4,6},{6,8},{8,10},{10,12},{12,14},{14,16},{16,18},{18... | collective-permute-start | bytes 3145736 | tf_op jit(solution)/shard_map/ppermute | solution.py:23
  11.2 1.1 pad_maximum_fusion.2
  12.2 1.9 %collective-permute-start.4 = (bf16[1024,512]{1,0:T(8,128)(2,1)}, bf16[1024,512]{1,0:T(8,128)(2,1)}, u32[]{:S(2)}, u32[]{:S(2)}) collective-permute-start(bf16[1024,512]{1,0:T(8,128)(2,1)} %pad_maximum_fusion.2), channel_id=1, source_target_pairs={{2,0},{4,2},{6,4},{8,6},{10,8},{12,10},{14,12},{16,14},{18,16},{20... | collective-permute-start | bytes 3145736 | tf_op jit(solution)/shard_map/ppermute | solution.py:23
  14.1 4.5 %collective-permute-start.3 = (bf16[1024,512]{1,0:T(8,128)(2,1)}, bf16[1024,512]{1,0:T(8,128)(2,1)}, u32[]{:S(2)}, u32[]{:S(2)}) collective-permute-start(bf16[1024,512]{1,0:T(8,128)(2,1)} %pad_maximum_fusion.2), channel_id=1, source_target_pairs={{0,2},{2,4},{4,6},{6,8},{8,10},{10,12},{12,14},{14,16},{16,18},{18... | collective-permute-start | bytes 3145736 | tf_op jit(solution)/shard_map/ppermute | solution.py:23
  18.7 0.1 dynamic_slice.7.active
  18.8 0.1 constant_dynamic-slice_fusion
  18.9 0.1 copy.13
  18.9 0.1 reshape.11.places
  19.0 6.0 %collective-permute-done = bf16[1024,512]{1,0:T(8,128)(2,1)S(1)} collective-permute-done((bf16[1024,512]{1,0:T(8,128)(2,1)}, bf16[1024,512]{1,0:T(8,128)(2,1)S(1)}, u32[]{:S(2)}, u32[]{:S(2)}) %collective-permute-start) | collective-permute-done | bytes 1048608 | tf_op jit(solution)/shard_map/ppermute | solution.py:428
  25.1 0.1 broadcast_select_fusion.1
  25.2 1.3 convolution_convert_fusion.refs_2_.refs_3_
  26.5 25.3 %shard_map.102 = (bf16[1024,256]{1,0:T(8,128)(2,1)S(1)}, bf16[1024,256]{1,0:T(8,128)(2,1)S(1)}, bf16[1024,512]{1,0:T(8,128)(2,1)S(1)}, f32[1024,512]{1,0:T(8,128)}, bf16[1024,512]{1,0:T(8,128)(2,1)S(1)}) custom-call(s32[96]{0:T(128)S(1)} %reshape.11.places, s32[8]{0:T(128)S(1)} %dynamic_slice.7.active, bf16[1024,512]{1,0:T(8,128)(2,1)S(1)} %copy-done.1, ...), custom_call_target="tpu_custom_call" | custom-call | flops 11274289152 | bytes 8388608 | tf_op jit(solution)/shard_map/pallas_call | solution.py:237
  51.8 16.3 %collective-permute-start.5 = (bf16[1024,512]{1,0:T(8,128)(2,1)S(1)}, bf16[1024,512]{1,0:T(8,128)(2,1)S(1)}, u32[]{:S(2)}, u32[]{:S(2)}) collective-permute-start(bf16[1024,512]{1,0:T(8,128)(2,1)S(1)} %get-tuple-element.17), channel_id=1, source_target_pairs={{2,0},{4,2},{6,4},{8,6},{10,8},{12,10},{14,12},{16,14},{18,16},{20... | collective-permute-start | bytes 3145736 | tf_op jit(solution)/shard_map/ppermute | solution.py:23
  68.1 1.9 %collective-permute-start.6 = (bf16[1024,512]{1,0:T(8,128)(2,1)S(1)}, bf16[1024,512]{1,0:T(8,128)(2,1)S(1)}, u32[]{:S(2)}, u32[]{:S(2)}) collective-permute-start(bf16[1024,512]{1,0:T(8,128)(2,1)S(1)} %get-tuple-element.18), channel_id=1, source_target_pairs={{0,2},{2,4},{4,6},{6,8},{8,10},{10,12},{12,14},{14,16},{16,18},{18... | collective-permute-start | bytes 3145736 | tf_op jit(solution)/shard_map/ppermute | solution.py:23
  70.1 25.2 %shard_map.103 = (bf16[1024,256]{1,0:T(8,128)(2,1)S(1)}, bf16[1024,256]{1,0:T(8,128)(2,1)S(1)}, bf16[1024,512]{1,0:T(8,128)(2,1)S(1)}, f32[1024,512]{1,0:T(8,128)}, bf16[1024,512]{1,0:T(8,128)(2,1)S(1)}) custom-call(s32[96]{0:T(128)S(1)} %reshape.11.places, s32[8]{0:T(128)S(1)} %dynamic_slice.7.active, bf16[1024,512]{1,0:T(8,128)(2,1)S(1)} %copy-done.1, ...), custom_call_target="tpu_custom_call" | custom-call | flops 11274289152 | bytes 8388608 | tf_op jit(solution)/shard_map/pallas_call | solution.py:237
  95.3 1.9 %collective-permute-start.7 = (bf16[1024,512]{1,0:T(8,128)(2,1)S(1)}, bf16[1024,512]{1,0:T(8,128)(2,1)S(1)}, u32[]{:S(2)}, u32[]{:S(2)}) collective-permute-start(bf16[1024,512]{1,0:T(8,128)(2,1)S(1)} %get-tuple-element.20), channel_id=1, source_target_pairs={{2,0},{4,2},{6,4},{8,6},{10,8},{12,10},{14,12},{16,14},{18,16},{20... | collective-permute-start | bytes 3145736 | tf_op jit(solution)/shard_map/ppermute | solution.py:23
  97.2 16.7 %collective-permute-start.8 = (bf16[1024,512]{1,0:T(8,128)(2,1)S(1)}, bf16[1024,512]{1,0:T(8,128)(2,1)S(1)}, u32[]{:S(2)}, u32[]{:S(2)}) collective-permute-start(bf16[1024,512]{1,0:T(8,128)(2,1)S(1)} %get-tuple-element.21), channel_id=1, source_target_pairs={{0,2},{2,4},{4,6},{6,8},{8,10},{10,12},{12,14},{14,16},{16,18},{18... | collective-permute-start | bytes 3145736 | tf_op jit(solution)/shard_map/ppermute | solution.py:23
  113.9 0.7 fusion.1.refs_0_
  114.6 0.7 fusion.refs_1_
  115.3 44.7 %shard_map.104 = bf16[512,1024]{1,0:T(8,128)(2,1)S(1)} custom-call(f32[256,1024]{1,0:T(8,128)S(1)} %fusion.1.refs_0_, f32[256,1024]{1,0:T(8,128)S(1)} %fusion.refs_1_), custom_call_target="tpu_custom_call" | custom-call | flops 2097152 | bytes 20971520 | tf_op jit(solution)/shard_map/pallas_call | solution.py:389
  160.0 1.1 pad_maximum_fusion.3
  161.1 1.6 convert_multiply_fusion
  162.7 0.7 copy-done.2
  163.4 0.4 add_convert_fusion.1
  164.0 1.5 copy-done.3
  165.5 0.4 add_convert_fusion
  166.0 1.1 pad_maximum_fusion.5
  167.0 1.1 pad_maximum_fusion.4
  (23 shorter events, 0.2 us)
Async XLA Ops:
  0.6 24.6 %copy-start = (bf16[512,1024]{1,0:T(8,128)(2,1)S(1)}, bf16[512,1024]{1,0:T(8,128)(2,1)}, u32[]{:S(2)}) copy-start(bf16[512,1024]{1,0:T(8,128)(2,1)} %param.11) | copy-start | bytes 3145732
  0.6 24.4 %collective-permute-start = (bf16[1024,512]{1,0:T(8,128)(2,1)}, bf16[1024,512]{1,0:T(8,128)(2,1)S(1)}, u32[]{:S(2)}, u32[]{:S(2)}) collective-permute-start(bf16[1024,512]{1,0:T(8,128)(2,1)} %param.10), channel_id=1, source_target_pairs={{0,1},{1,0},{2,3},{3,2},{4,5},{5,4},{6,7},{7,6},{8,9},{9,8},{10,11... | collective-permute-start | bytes 3145736 | tf_op jit(solution)/shard_map/ppermute | solution.py:428
  3.6 15.1 %copy-start.6 = (s32[128]{0:T(128)S(1)}, s32[128]{0:T(128)}, u32[]{:S(2)}) copy-start(s32[128]{0:T(128)} %param.13) | copy-start | bytes 1540
  3.6 15.2 %copy-start.5 = (s32[128,12]{0,1:T(8,128)S(1)}, s32[128,12]{0,1:T(8,128)}, u32[]{:S(2)}) copy-start(s32[128,12]{0,1:T(8,128)} %param.12) | copy-start | bytes 18436
  3.6 21.4 %copy-start.4 = (bf16[1024,512]{1,0:T(8,128)(2,1)S(1)}, bf16[1024,512]{1,0:T(8,128)(2,1)}, u32[]{:S(2)}) copy-start(bf16[1024,512]{1,0:T(8,128)(2,1)} %param.10) | copy-start | bytes 3145732
  4.7 21.8 %collective-permute-start.2 = (bf16[1024,512]{1,0:T(8,128)(2,1)}, bf16[1024,512]{1,0:T(8,128)(2,1)}, u32[]{:S(2)}, u32[]{:S(2)}) collective-permute-start(bf16[1024,512]{1,0:T(8,128)(2,1)} %pad_maximum_fusion.1), channel_id=1, source_target_pairs={{2,0},{4,2},{6,4},{8,6},{10,8},{12,10},{14,12},{16,14},{18,16},{20... | collective-permute-start | bytes 3145736 | tf_op jit(solution)/shard_map/ppermute | solution.py:23
  7.6 19.0 %collective-permute-start.1 = (bf16[1024,512]{1,0:T(8,128)(2,1)}, bf16[1024,512]{1,0:T(8,128)(2,1)}, u32[]{:S(2)}, u32[]{:S(2)}) collective-permute-start(bf16[1024,512]{1,0:T(8,128)(2,1)} %pad_maximum_fusion.1), channel_id=1, source_target_pairs={{0,2},{2,4},{4,6},{6,8},{8,10},{10,12},{12,14},{14,16},{16,18},{18... | collective-permute-start | bytes 3145736 | tf_op jit(solution)/shard_map/ppermute | solution.py:23
  12.2 57.8 %collective-permute-start.4 = (bf16[1024,512]{1,0:T(8,128)(2,1)}, bf16[1024,512]{1,0:T(8,128)(2,1)}, u32[]{:S(2)}, u32[]{:S(2)}) collective-permute-start(bf16[1024,512]{1,0:T(8,128)(2,1)} %pad_maximum_fusion.2), channel_id=1, source_target_pairs={{2,0},{4,2},{6,4},{8,6},{10,8},{12,10},{14,12},{16,14},{18,16},{20... | collective-permute-start | bytes 3145736 | tf_op jit(solution)/shard_map/ppermute | solution.py:23
  14.1 55.9 %collective-permute-start.3 = (bf16[1024,512]{1,0:T(8,128)(2,1)}, bf16[1024,512]{1,0:T(8,128)(2,1)}, u32[]{:S(2)}, u32[]{:S(2)}) collective-permute-start(bf16[1024,512]{1,0:T(8,128)(2,1)} %pad_maximum_fusion.2), channel_id=1, source_target_pairs={{0,2},{2,4},{4,6},{6,8},{8,10},{10,12},{12,14},{14,16},{16,18},{18... | collective-permute-start | bytes 3145736 | tf_op jit(solution)/shard_map/ppermute | solution.py:23
  25.2 1.3 copy-start.1
  51.8 110.8 %collective-permute-start.5 = (bf16[1024,512]{1,0:T(8,128)(2,1)S(1)}, bf16[1024,512]{1,0:T(8,128)(2,1)S(1)}, u32[]{:S(2)}, u32[]{:S(2)}) collective-permute-start(bf16[1024,512]{1,0:T(8,128)(2,1)S(1)} %get-tuple-element.17), channel_id=1, source_target_pairs={{2,0},{4,2},{6,4},{8,6},{10,8},{12,10},{14,12},{16,14},{18,16},{20... | collective-permute-start | bytes 3145736 | tf_op jit(solution)/shard_map/ppermute | solution.py:23
  68.1 94.6 %collective-permute-start.6 = (bf16[1024,512]{1,0:T(8,128)(2,1)S(1)}, bf16[1024,512]{1,0:T(8,128)(2,1)S(1)}, u32[]{:S(2)}, u32[]{:S(2)}) collective-permute-start(bf16[1024,512]{1,0:T(8,128)(2,1)S(1)} %get-tuple-element.18), channel_id=1, source_target_pairs={{0,2},{2,4},{4,6},{6,8},{8,10},{10,12},{12,14},{14,16},{16,18},{18... | collective-permute-start | bytes 3145736 | tf_op jit(solution)/shard_map/ppermute | solution.py:23
  95.3 68.7 %collective-permute-start.7 = (bf16[1024,512]{1,0:T(8,128)(2,1)S(1)}, bf16[1024,512]{1,0:T(8,128)(2,1)S(1)}, u32[]{:S(2)}, u32[]{:S(2)}) collective-permute-start(bf16[1024,512]{1,0:T(8,128)(2,1)S(1)} %get-tuple-element.20), channel_id=1, source_target_pairs={{2,0},{4,2},{6,4},{8,6},{10,8},{12,10},{14,12},{16,14},{18,16},{20... | collective-permute-start | bytes 3145736 | tf_op jit(solution)/shard_map/ppermute | solution.py:23
  97.2 66.8 %collective-permute-start.8 = (bf16[1024,512]{1,0:T(8,128)(2,1)S(1)}, bf16[1024,512]{1,0:T(8,128)(2,1)S(1)}, u32[]{:S(2)}, u32[]{:S(2)}) collective-permute-start(bf16[1024,512]{1,0:T(8,128)(2,1)S(1)} %get-tuple-element.21), channel_id=1, source_target_pairs={{0,2},{2,4},{4,6},{6,8},{8,10},{10,12},{12,14},{14,16},{16,18},{18... | collective-permute-start | bytes 3145736 | tf_op jit(solution)/shard_map/ppermute | solution.py:23
  161.1 2.3 %copy-start.2 = (f32[1024,512]{1,0:T(8,128)S(1)}, f32[1024,512]{1,0:T(8,128)}, u32[]{:S(2)}) copy-start(f32[1024,512]{1,0:T(8,128)} %get-tuple-element.16) | copy-start | bytes 6291460
  163.9 1.6 copy-start.3
